TPU v7x, 32 devices: a whole 2x2x4 slice. The times are simulated.
32 devices in a mesh: dp: 16 (over z, y, core), mp: 2 (over x).
Axes of the slice: x: 2, y: 2, z: 4, core: 2. Of those that a mesh axis runs over, the one named last changes fastest.
Arguments:
- tokens: bfloat16 [16384, 768], P('dp'), may hold values from -6 to 6
- document_lengths: int32 [1, 8], replicated, may hold values from 0 to 16384, as said below
- feature_maps: bfloat16 [12, 64, 256], replicated, may hold values from -5 to 5
- joint_weight: bfloat16 [768, 2304], P(('dp', 'mp')), may hold values from -0.21875 to 0.21875
- joint_bias: bfloat16 [2304], P(('dp', 'mp')), may hold values from -1.25 to 1.25
- output_weight: bfloat16 [768, 768], P(('dp', 'mp')), may hold values from -1.75 to 1.75
- output_bias: bfloat16 [768], P(('dp', 'mp')), may hold values from -1.25 to 1.25
- first_gain: bfloat16 [768], P(('dp', 'mp')), may hold values from 0.25 to 1.75
- first_shift: bfloat16 [768], P(('dp', 'mp')), may hold values from -1.25 to 1.25
- up_weight: bfloat16 [768, 3072], P(None, 'mp'), may hold values from -0.21875 to 0.21875
- up_bias: bfloat16 [3072], P('mp'), may hold values from -1.25 to 1.25
- down_weight: bfloat16 [3072, 768], P('mp'), may hold values from -0.109375 to 0.109375
- down_bias: bfloat16 [768], replicated, may hold values from -1.25 to 1.25
- second_gain: bfloat16 [768], P(('dp', 'mp')), may hold values from 0.25 to 1.75
- second_shift: bfloat16 [768], P(('dp', 'mp')), may hold values from -1.25 to 1.25
- cotangent: bfloat16 [16384, 768], P('dp'), may hold values from -6 to 6
Outputs:
- layer_output: bfloat16 [16384, 768], P('dp')
- tokens_grad: bfloat16 [16384, 768], P('dp')
- joint_weight_grad: float32 [768, 2304], P(('dp', 'mp'))
- joint_bias_grad: float32 [2304], P(('dp', 'mp'))
- output_weight_grad: float32 [768, 768], P(('dp', 'mp'))
- output_bias_grad: float32 [768], P(('dp', 'mp'))
- first_gain_grad: float32 [768], P(('dp', 'mp'))
- first_shift_grad: float32 [768], P(('dp', 'mp'))
- up_weight_grad: float32 [768, 3072], P(None, 'mp')
- up_bias_grad: float32 [3072], P('mp')
- down_weight_grad: float32 [3072, 768], P('mp')
- down_bias_grad: float32 [768], replicated
- second_gain_grad: float32 [768], P(('dp', 'mp'))
- second_shift_grad: float32 [768], P(('dp', 'mp'))
Inputs may be any that keep to these rules, and one draw needn't show every extreme that they name: `document_lengths`: each row of 16384 positions holds its 8 documents in order from its first position, then padding. In every row one document has more than 15360 tokens and the others together with the padding fewer than 1024.
All inputs are finite; a program needn't handle non-finite values.
Results may differ from a plain program's by a relative error of at most 0.033.
Values may be sent and summed in bfloat16 or wider, within the bound.
No kernel may reach another device: no remote copies, remote signals or barrier semaphores. Data moves between devices by JAX's collectives and lax.ppermute only.
A program may use at most 576 MiB of HBM per device.

v0:
```python
from functools import partial
import math

import jax
import jax.numpy as jnp
from jax import lax
from jax.experimental import pallas as pl
from jax.experimental.pallas import tpu as pltpu
from jax.sharding import PartitionSpec as P

EPSILON = 1e-05
F32 = jnp.float32
BF16 = jnp.bfloat16
LOG2E = math.log2(math.e)
VMEM_LIMIT = 56 * 1024 * 1024
SLOTS = 8
WINDOW = 128
EXTRA = 32
TILE = 256


def nn(a, b):
    return lax.dot_general(a, b, (((1,), (0,)), ((), ())), preferred_element_type=F32)


def nt(a, b):
    return lax.dot_general(a, b, (((1,), (1,)), ((), ())), preferred_element_type=F32)


def tn(a, b):
    return lax.dot_general(a, b, (((0,), (0,)), ((), ())), preferred_element_type=F32)


def fold_rows(a):
    return jnp.sum(a.reshape(a.shape[0] // 8, 8, a.shape[1]), axis=0)


def after(value, *deps):
    return lax.optimization_barrier((value, deps))[0]


def dp_bits():
    count = lax.axis_size("dp")
    bits = []
    bit = count // 2
    while bit:
        bits.append(bit)
        bit //= 2
    return bits


def far_first():
    return dp_bits()


def near_first():
    bits = dp_bits()
    if len(bits) < 3:
        return bits
    return [bits[-2]] + bits[:-2] + [bits[-1]]


def swap_dp(a, bit):
    count = lax.axis_size("dp")
    return lax.ppermute(a, "dp", [(i, i ^ bit) for i in range(count)])


def swap_mp(a):
    return lax.ppermute(a, "mp", [(0, 1), (1, 0)])


def mine(bit):
    return (lax.axis_index("dp") // bit) % 2


def join_pair(own, other, bit, axis):
    low = jnp.stack([own, other], axis)
    high = jnp.stack([other, own], axis)
    return jnp.where(bit == 0, low, high)


class Gather:
    def __init__(self, a, order, done=()):
        self.a = a
        self.tail = a.shape[len(done) :]
        self.order = list(order)
        self.done = list(done)
        self.got = None

    def start(self, *deps):
        if deps:
            self.a = after(self.a, *deps)
        self.got = swap_dp(self.a, self.order[0])
        return self

    def finish(self, *deps):
        bit = self.order.pop(0)
        got = after(self.got, *deps) if deps else self.got
        place = sum(1 for d in self.done if d > bit)
        self.a = join_pair(self.a, got, mine(bit), place)
        self.done.append(bit)
        return self

    def rest(self):
        while self.order:
            self.start().finish()
        return self.result()

    def result(self):
        return self.a.reshape((-1,) + self.tail[1:])


class Scatter:
    def __init__(self, a, order):
        count = lax.axis_size("dp")
        self.left = dp_bits()
        self.a = a.reshape((2,) * len(self.left) + (a.shape[0] // count,) + a.shape[1:])
        self.order = list(order)

    def start(self, *deps):
        bit = self.order[0]
        axis = self.left.index(bit)
        a = after(self.a, *deps) if deps else self.a
        self.own = lax.dynamic_index_in_dim(a, mine(bit), axis, False)
        self.got = swap_dp(lax.dynamic_index_in_dim(a, 1 - mine(bit), axis, False), bit)
        return self

    def finish(self, *deps):
        self.left.remove(self.order.pop(0))
        got = after(self.got, *deps) if deps else self.got
        self.a = (self.own.astype(F32) + got.astype(F32)).astype(self.a.dtype)
        return self

    def rest(self):
        while self.order:
            self.start().finish()
        return self.a

    def start_swap(self, *deps):
        self.own = after(self.a, *deps) if deps else self.a
        self.bit = self.left[0]
        self.got = swap_dp(self.own, self.bit)
        return self

    def finish_swap(self, *deps):
        got = after(self.got, *deps) if deps else self.got
        self.a = (self.own.astype(F32) + got.astype(F32)).astype(self.a.dtype)
        return self

    def gather(self, order):
        return Gather(self.a, order, self.left)


class TableSum:
    def __init__(self, packed):
        self.core = mine(1)
        self.shape = packed.shape
        halves = packed.reshape(2, packed.shape[0] // 2, packed.shape[1])
        self.own = lax.dynamic_index_in_dim(halves, self.core, 0, False)
        self.got = swap_dp(lax.dynamic_index_in_dim(halves, 1 - self.core, 0, False), 1)

    def add(self, *deps):
        got = after(self.got, *deps) if deps else self.got
        self.own = (self.own.astype(F32) + got.astype(F32)).astype(self.own.dtype)
        return self

    def swap(self, bit):
        self.got = swap_dp(self.own, bit)
        return self

    def join(self, *deps):
        got = after(self.got, *deps) if deps else self.got
        return join_pair(self.own, got, self.core, 0).reshape(self.shape)


def full(shape):
    return pl.BlockSpec(shape, lambda t, *_: (0,) * len(shape), pipeline_mode=pl.Buffered(1))


def column(shape, place):
    return pl.BlockSpec(shape, lambda t, *_: (0, place), pipeline_mode=pl.Buffered(1))


def rows(tile, width):
    return pl.BlockSpec((tile, width), lambda t, *_: (t, 0))


def held(shape):
    return pl.BlockSpec(shape, lambda t, *_: (0,) * len(shape))


def call(kernel, tiles, in_specs, outs, scratch, flops):
    return pl.pallas_call(
        kernel,
        grid_spec=pltpu.PrefetchScalarGridSpec(
            num_scalar_prefetch=1,
            grid=(tiles,),
            in_specs=in_specs,
            out_specs=[spec for spec, _, _ in outs],
            scratch_shapes=scratch,
        ),
        out_shape=[jax.ShapeDtypeStruct(shape, kind) for _, shape, kind in outs],
        compiler_params=pltpu.CompilerParams(
            vmem_limit_bytes=VMEM_LIMIT, dimension_semantics=("arbitrary",)
        ),
        cost_estimate=pl.CostEstimate(flops=int(flops), bytes_accessed=20_000_000, transcendentals=0),
    )


def features(scaled, table):
    lhs = jnp.concatenate([scaled.astype(BF16), (-0.5 * scaled * scaled).astype(BF16)], axis=1)
    return jnp.exp2(nn(lhs, table) * LOG2E - 4.0)


def each_small(flags, t, slot, body):
    limit = slot.shape[0] - WINDOW

    def one(j, carry):
        first = flags[t, j]
        final = flags[t, SLOTS + j]
        begin = first // 16 * 16

        def window(i, carry):
            wanted = begin + i * WINDOW
            start = pl.multiple_of(jnp.minimum(wanted, limit), 16)
            rows = pl.ds(start, WINDOW)
            index = lax.broadcasted_iota(jnp.int32, (WINDOW, 128), 0) + start
            body(rows, jnp.logical_and(slot[rows, :] == j, index >= wanted), j)
            return carry

        count = jnp.where(final > first, (final - begin + WINDOW - 1) // WINDOW, 0)
        lax.fori_loop(0, count, window, 0)
        return carry

    lax.fori_loop(1, SLOTS, one, 0)


def pack_tables(table, base, acc, macc):
    pairs = acc.shape[0]
    masses = []
    for p in range(pairs):
        for k in range(2):
            head = 2 * p + k
            span = slice(k * 256, (k + 1) * 256)
            table[pl.ds(base + head * 64, 64), :] = acc[p, k * 64 : (k + 1) * 64, span].astype(BF16)
            source = macc[p, :, span] if macc is not None else acc[p, 128 + k * 64 : 192 + k * 64, span]
            masses.append(jnp.sum(source, axis=0, keepdims=True))
    masses.append(jnp.zeros((16 - 2 * pairs, 256), F32))
    table[pl.ds(base + pairs * 128, 16), :] = jnp.concatenate(masses, axis=0).astype(BF16)


def fill_tables(tabs, main, repeat):
    pairs = tabs.shape[0]
    tabs[...] = jnp.zeros_like(tabs)
    masses = main[pl.ds(pairs * 128, 16), :].astype(F32)
    for p in range(pairs):
        for k in range(2):
            head = 2 * p + k
            span = slice(k * 256, (k + 1) * 256)
            tabs[p, k * 64 : (k + 1) * 64, span] = main[pl.ds(head * 64, 64), :]
            mass = jnp.broadcast_to(masses[head : head + 1, :], (64, 256))
            if not repeat:
                mass = jnp.where(lax.broadcasted_iota(jnp.int32, (64, 256), 0) == 0, mass, 0.0)
            tabs[p, 128 + k * 64 : 192 + k * 64, span] = mass.astype(BF16)


def copy_small(flags, source, target, sems):
    stride = source.shape[0] // (SLOTS - 1)

    def part(j):
        span = pl.ds((j - 1) * stride, stride)
        return pltpu.make_async_copy(source.at[span], target.at[span], sems.at[j - 1])

    for j in range(1, SLOTS):

        @pl.when(flags[0, 2 * SLOTS + j] > 0)
        def _():
            part(j).start()

    for j in range(1, SLOTS):

        @pl.when(flags[0, 2 * SLOTS + j] > 0)
        def _():
            part(j).wait()


def small_table(small, j, p, pairs, repeat, with_masses=True):
    stride = pairs * 128 + 16
    base = (j - 1) * stride
    zero = jnp.zeros((64, 256), BF16)
    tops, bottoms = [], []
    if with_masses:
        masses = small[pl.ds(pl.multiple_of(base + pairs * 128, 16), 16), :].astype(F32)
    for k in range(2):
        head = 2 * p + k
        top = small[pl.ds(pl.multiple_of(base + head * 64, 16), 64), :]
        tops.append(jnp.concatenate([top, zero] if k == 0 else [zero, top], axis=1))
        if with_masses:
            mass = jnp.broadcast_to(masses[head : head + 1, :], (64, 256))
            if not repeat:
                mass = jnp.where(lax.broadcasted_iota(jnp.int32, (64, 256), 0) == 0, mass, 0.0)
            mass = mass.astype(BF16)
            bottoms.append(jnp.concatenate([mass, zero] if k == 0 else [zero, mass], axis=1))
    return jnp.concatenate(tops + bottoms, axis=0)


def masked(mask, value):
    wide = jnp.concatenate([mask] * (value.shape[1] // 128), axis=1)
    return jnp.where(wide, value.astype(F32), 0.0)


def keys_kernel(
    flags, x, key_weight, value_weight, bias, table, slot,
    phi, values, scaled_out, main, small_out,
    acc, macc, sacc, smacc, small, sems,
):
    t = pl.program_id(0)
    pairs = table.shape[0]
    width = pairs * 128
    slow = flags[t, 0] == 0

    @pl.when(t == 0)
    def _():
        acc[...] = jnp.zeros_like(acc)
        macc[...] = jnp.zeros_like(macc)

        for j in range(1, SLOTS):

            @pl.when(flags[0, 2 * SLOTS + j] > 0)
            def _():
                sacc[j - 1] = jnp.zeros_like(sacc[j - 1])
                smacc[j - 1] = jnp.zeros_like(smacc[j - 1])

    keys = nn(x[...], key_weight[:, :width]) + bias[:, :width]
    values[...] = (nn(x[...], value_weight[...]) + bias[:, width:]).astype(BF16)
    for p in range(pairs):
        scaled = keys[:, p * 128 : (p + 1) * 128] * 64 ** (-0.25)
        scaled_out[:, p * 128 : (p + 1) * 128] = scaled.astype(BF16)
        phi[:, p * 512 : (p + 1) * 512] = features(scaled, table[p]).astype(BF16)

    @pl.when(jnp.logical_not(slow))
    def _():
        for p in range(pairs):
            part = phi[:, p * 512 : (p + 1) * 512]
            acc[p] += tn(values[:, p * 128 : (p + 1) * 128], part)
            macc[p] += fold_rows(part.astype(F32))

    @pl.when(slow)
    def _():
        mask = slot[...] == 0
        for p in range(pairs):
            part = phi[:, p * 512 : (p + 1) * 512]
            acc[p] += tn(masked(mask, values[:, p * 128 : (p + 1) * 128]).astype(BF16), part)
            macc[p] += fold_rows(masked(mask, part))

        def body(rows, mask, j):
            for p in range(pairs):
                part = phi[rows, p * 512 : (p + 1) * 512]
                value = masked(mask, values[rows, p * 128 : (p + 1) * 128]).astype(BF16)
                sacc[j - 1, p] += tn(value, part)
                smacc[j - 1, p] += fold_rows(masked(mask, part))

        each_small(flags, t, slot, body)

    @pl.when(t == pl.num_programs(0) - 1)
    def _():
        pack_tables(main, 0, acc, macc)

        for j in range(1, SLOTS):

            @pl.when(flags[0, 2 * SLOTS + j] > 0)
            def _():
                pack_tables(small, (j - 1) * main.shape[0], sacc.at[j - 1], smacc.at[j - 1])

        copy_small(flags, small, small_out, sems)


def queries_kernel(flags, x, weight, bias, table, select, phi, scaled_out, chosen):
    pairs = table.shape[0]
    query = nn(x[...], weight[...]) + bias[...]
    chosen[...] = nn(x[...], select[...]).astype(BF16)
    for p in range(pairs):
        scaled = query[:, p * 128 : (p + 1) * 128] * 64 ** (-0.25)
        scaled_out[:, p * 128 : (p + 1) * 128] = scaled.astype(BF16)
        phi[:, p * 512 : (p + 1) * 512] = features(scaled, table[p]).astype(BF16)


def center(z):
    average = jnp.mean(z, axis=1, keepdims=True)
    centered = z - average
    inverse = lax.rsqrt(jnp.mean(centered * centered, axis=1, keepdims=True) + EPSILON)
    return centered * inverse, inverse


def center_back(e, normed, inverse):
    first = jnp.mean(e, axis=1, keepdims=True)
    second = jnp.mean(e * normed, axis=1, keepdims=True)
    return inverse * (e - first - normed * second)


def middle_kernel(
    flags, x, cot, slot, phi, main, small_in,
    out_weight, up_own, up_here, up_there, down_own, down_here, down_there, bias_own, bias_other, vectors,
    layer_out, hidden_grad, normed_out, inverse_out, att_out, invden_out,
    active_out, dup_out, hidden_out, dffn_out, sums, up_sum,
    tabs, spread, gates, other, up_other, down_other, small, sems, half_sems,
):
    t = pl.program_id(0)
    pairs = tabs.shape[0]
    width = pairs * 128
    core = flags[0, 3 * SLOTS]

    def halves():
        copies = []
        for target, here, there in [(up_other, up_here, up_there), (down_other, down_here, down_there)]:
            count = here.shape[0]
            for source, place in [(here, core), (there, 1 - core)]:
                span = pl.ds(pl.multiple_of(place * count, count), count)
                copies.append((source, target.at[span]))
        return [
            pltpu.make_async_copy(source, target, half_sems.at[i])
            for i, (source, target) in enumerate(copies)
        ]

    @pl.when(t == 0)
    def _():
        for copy in halves():
            copy.start()
        fill_tables(tabs, main, True)
        copy_small(flags, small_in, small, sems)
        sums[...] = jnp.zeros_like(sums)
        up_sum[...] = jnp.zeros_like(up_sum)

    for p in range(pairs):
        spread[:, p * 256 : (p + 1) * 256] = nt(phi[:, p * 512 : (p + 1) * 512], tabs[p])

    @pl.when(flags[t, 0] == 0)
    def _():
        def body(rows, mask, j):
            wide = jnp.concatenate([mask] * 2, axis=1)
            for p in range(pairs):
                got = nt(phi[rows, p * 512 : (p + 1) * 512], small_table(small, j, p, pairs, True))
                old = spread[rows, p * 256 : (p + 1) * 256]
                spread[rows, p * 256 : (p + 1) * 256] = jnp.where(wide, got, old)

        each_small(flags, t, slot, body)

    live = slot[...] < SLOTS
    for p in range(pairs):
        numerator = spread[:, p * 256 : p * 256 + 128]
        denominator = spread[:, p * 256 + 128 : (p + 1) * 256]
        inverse = jnp.where(live, 1.0 / jnp.where(live, denominator, 1.0), 0.0)
        invden_out[:, p * 128 : (p + 1) * 128] = inverse
        att_out[:, p * 128 : (p + 1) * 128] = (numerator * inverse).astype(BF16)

    def vector(i):
        return vectors[i : i + 1, :]

    branch = nn(att_out[...], out_weight[...]) + vector(0)
    first, first_inverse = center(x[...].astype(F32) + branch)
    normed_out[...] = first
    inverse_out[...] = jnp.broadcast_to(first_inverse, inverse_out.shape)
    hidden = first * vector(1) + vector(2)
    hidden_low = hidden.astype(BF16)
    hidden_out[...] = hidden_low
    step = 512
    half = up_own.shape[1]

    @pl.when(t == 0)
    def _():
        for copy in halves():
            copy.wait()

    for which, (up, bias, act) in enumerate(
        [(up_own, bias_own, active_out), (up_other, bias_other, other)]
    ):
        for c in range(0, half, step):
            value = nn(hidden_low, up[:, c : c + step]) + bias[:, c : c + step]
            cdf = 0.5 + 0.5 * lax.erf(value * math.sqrt(0.5))
            gates[:, which * half + c : which * half + c + step] = cdf + value * jnp.exp2(
                value * value * (-0.5 * LOG2E)
            ) * (1.0 / math.sqrt(2.0 * math.pi))
            act[:, c : c + step] = (value * cdf).astype(BF16)
    total = hidden + vector(3)
    total = total + nn(active_out[...], down_own[...])
    total = total + nn(other[...], down_other[...])
    second, second_inverse = center(total)
    layer_out[...] = (second * vector(4) + vector(5)).astype(BF16)
    g = cot[...].astype(F32)
    sums[0:8, :] += fold_rows(g * second)
    sums[8:16, :] += fold_rows(g)
    dsecond = center_back(g * vector(4), second, second_inverse)
    dffn = dsecond.astype(BF16)
    dffn_out[...] = dffn
    sums[16:24, :] += fold_rows(dffn.astype(F32))
    for which, (down, dup_ref) in enumerate([(down_own, dup_out), (down_other, other)]):
        for c in range(0, half, step):
            gate = gates[:, which * half + c : which * half + c + step]
            dup = (nt(dffn, down[c : c + step, :]) * gate).astype(BF16)
            dup_ref[:, c : c + step] = dup
            if which == 0:
                up_sum[:, c : c + step] += fold_rows(dup.astype(F32))
    dsecond = dsecond + nt(dup_out[...], up_own[...])
    dsecond = dsecond + nt(other[...], up_other[...])
    hidden_grad[...] = dsecond


def attention_back_kernel(
    flags, hidden_grad, normed, inverse, att, invden, phi, slot, out_weight, gain, select, more, up_sum,
    dfirst_out, dbranch_out, mixed, chosen, sums, main, small_out,
    acc, sacc, small, sems,
):
    t = pl.program_id(0)
    pairs = acc.shape[0]
    slow = flags[t, 0] == 0

    @pl.when(t == 0)
    def _():
        acc[...] = jnp.zeros_like(acc)
        sums[...] = jnp.zeros_like(sums)

        for j in range(1, SLOTS):

            @pl.when(flags[0, 2 * SLOTS + j] > 0)
            def _():
                sacc[j - 1] = jnp.zeros_like(sacc[j - 1])

    grad = hidden_grad[...]
    first = normed[...]
    sums[0:8, :] += fold_rows(grad * first)
    sums[8:16, :] += fold_rows(grad)
    dfirst = center_back(grad * gain[...], first, inverse[:, 0:1])
    dfirst_out[...] = dfirst
    dbranch = dfirst.astype(BF16)
    dbranch_out[...] = dbranch
    sums[16:24, :] += fold_rows(dbranch.astype(F32))
    chosen[...] = nn(att[...], select[...]).astype(BF16)
    datt = nt(dbranch, out_weight[...])
    ratio = datt * invden[...]
    dden = -ratio * att[...].astype(F32)
    for p in range(pairs):
        mixed[:, p * 256 : p * 256 + 128] = ratio[:, p * 128 : (p + 1) * 128].astype(BF16)
        mixed[:, p * 256 + 128 : (p + 1) * 256] = dden[:, p * 128 : (p + 1) * 128].astype(BF16)

    @pl.when(jnp.logical_not(slow))
    def _():
        for p in range(pairs):
            acc[p] += tn(mixed[:, p * 256 : (p + 1) * 256], phi[:, p * 512 : (p + 1) * 512])

    @pl.when(slow)
    def _():
        mask = slot[...] == 0
        for p in range(pairs):
            part = masked(mask, mixed[:, p * 256 : (p + 1) * 256]).astype(BF16)
            acc[p] += tn(part, phi[:, p * 512 : (p + 1) * 512])

        def body(rows, mask, j):
            for p in range(pairs):
                part = masked(mask, mixed[rows, p * 256 : (p + 1) * 256]).astype(BF16)
                sacc[j - 1, p] += tn(part, phi[rows, p * 512 : (p + 1) * 512])

        each_small(flags, t, slot, body)

    @pl.when(t == pl.num_programs(0) - 1)
    def _():
        pack_tables(main, 0, acc, None)
        lines = []
        for source in (sums, more, up_sum):
            for i in range(source.shape[0] // 8):
                line = jnp.sum(source[8 * i : 8 * i + 8, :], axis=0, keepdims=True)
                lines += [line[:, c : c + 256] for c in range(0, source.shape[1], 256)]
        lines.append(jnp.zeros((EXTRA - len(lines), 256), F32))
        main[pl.ds(pairs * 128 + 16, EXTRA), :] = jnp.concatenate(lines, axis=0).astype(BF16)

        for j in range(1, SLOTS):

            @pl.when(flags[0, 2 * SLOTS + j] > 0)
            def _():
                pack_tables(small, (j - 1) * (pairs * 128 + 16), sacc.at[j - 1], None)

        copy_small(flags, small, small_out, sems)


def feature_back(rows, p, grad, phi, scaled, table):
    span = slice(p * 128, (p + 1) * 128)
    e = (grad * phi[rows, p * 512 : (p + 1) * 512].astype(F32)).astype(BF16)
    back = nt(e, table[p])
    return (back[:, :128] - scaled[rows, span].astype(F32) * back[:, 128:]) * 64 ** (-0.25)


def store_some(ref, rows, span, mask, value):
    old = ref[rows, span].astype(F32)
    ref[rows, span] = jnp.where(mask, value, old).astype(ref.dtype)


def queries_back_kernel(
    flags, mixed, phi, scaled, slot, main, small_in, table, weight, dfirst,
    dquery_out, partial_out, sums, tabs, small, sems,
):
    t = pl.program_id(0)
    pairs = tabs.shape[0]

    @pl.when(t == 0)
    def _():
        fill_tables(tabs, main, True)
        copy_small(flags, small_in, small, sems)
        sums[...] = jnp.zeros_like(sums)

    for p in range(pairs):
        grad = nn(mixed[:, p * 256 : (p + 1) * 256], tabs[p])
        du = feature_back(slice(None), p, grad, phi, scaled, table)
        dquery_out[:, p * 128 : (p + 1) * 128] = du.astype(BF16)

    @pl.when(flags[t, 0] == 0)
    def _():
        def body(rows, mask, j):
            for p in range(pairs):
                own = small_table(small, j, p, pairs, True)
                grad = nn(mixed[rows, p * 256 : (p + 1) * 256], own)
                du = feature_back(rows, p, grad, phi, scaled, table)
                store_some(dquery_out, rows, slice(p * 128, (p + 1) * 128), mask, du)

        each_small(flags, t, slot, body)

    sums[...] += fold_rows(dquery_out[...].astype(F32))
    partial_out[...] = dfirst[...] + nt(dquery_out[...], weight[...])


def keys_back_kernel(
    flags, phi, values, scaled, slot, main, small_in, table, key_weight, value_weight, partial_in,
    djoint_out, tokens_out, sums, tabs, small, sems,
):
    t = pl.program_id(0)
    pairs = tabs.shape[0]
    width = pairs * 128

    @pl.when(t == 0)
    def _():
        fill_tables(tabs, main, False)
        copy_small(flags, small_in, small, sems)
        sums[...] = jnp.zeros_like(sums)

    def extended(rows, p):
        value = values[rows, p * 128 : (p + 1) * 128]
        return jnp.concatenate([value, jnp.ones_like(value)], axis=1)

    for p in range(pairs):
        grad = nn(extended(slice(None), p), tabs[p])
        du = feature_back(slice(None), p, grad, phi, scaled, table)
        djoint_out[:, p * 128 : (p + 1) * 128] = du.astype(BF16)
        dvalue = nt(phi[:, p * 512 : (p + 1) * 512], tabs[p, :128, :])
        djoint_out[:, width + p * 128 : width + (p + 1) * 128] = dvalue.astype(BF16)

    @pl.when(flags[t, 0] == 0)
    def _():
        live = slot[...] < SLOTS
        for p in range(2 * pairs):
            part = djoint_out[:, p * 128 : (p + 1) * 128]
            djoint_out[:, p * 128 : (p + 1) * 128] = masked(live, part).astype(BF16)

        def body(rows, mask, j):
            for p in range(pairs):
                own = small_table(small, j, p, pairs, False)
                grad = nn(extended(rows, p), own)
                du = feature_back(rows, p, grad, phi, scaled, table)
                store_some(djoint_out, rows, slice(p * 128, (p + 1) * 128), mask, du)
                dvalue = nt(phi[rows, p * 512 : (p + 1) * 512], own[:128, :])
                span = slice(width + p * 128, width + (p + 1) * 128)
                store_some(djoint_out, rows, span, mask, dvalue)

        each_small(flags, t, slot, body)

    sums[...] += fold_rows(djoint_out[...].astype(F32))
    tokens_out[...] = (
        partial_in[...]
        + nt(djoint_out[:, :width], key_weight[:, :width])
        + nt(djoint_out[:, width:], value_weight[...])
    ).astype(BF16)


def table_outs(width, extra=0):
    count = width + 16
    small = (SLOTS - 1) * count
    count = count + extra
    anywhere = pl.BlockSpec(memory_space=pl.ANY)
    return [(held((count, 256)), (count, 256), BF16), (anywhere, (small, 256), BF16)]


def table_ins(width):
    return [full((width + 16, 256)), pl.BlockSpec(memory_space=pl.ANY)]


def table_scratch(width):
    return pltpu.VMEM((width // 128, 256, 512), BF16)


def small_scratch(width):
    return pltpu.VMEM(((SLOTS - 1) * (width + 16), 256), BF16)


def run_keys(tile, flags, tokens, key_weight, value_weight, bias, table, slots):
    count, width = tokens.shape
    pairs = table.shape[0]
    wide = pairs * 512
    return call(
        keys_kernel,
        count // tile,
        [
            rows(tile, width), full(key_weight.shape), full((width, width)), full((1, 2 * width)),
            full(table.shape), rows(tile, 128),
        ],
        [
            (rows(tile, wide), (count, wide), BF16),
            (rows(tile, width), (count, width), BF16),
            (rows(tile, width), (count, width), BF16),
        ]
        + table_outs(width),
        [
            pltpu.VMEM((pairs, 128, 512), F32),
            pltpu.VMEM((pairs, 8, 512), F32),
            pltpu.VMEM((SLOTS - 1, pairs, 128, 512), F32),
            pltpu.VMEM((SLOTS - 1, pairs, 8, 512), F32),
            small_scratch(width),
            pltpu.SemaphoreType.DMA((SLOTS - 1,)),
        ],
        10e9,
    )(flags, tokens, key_weight, value_weight, bias, table, slots)


def run_queries(tile, flags, tokens, weight, bias, table, select):
    count, width = tokens.shape
    wide = table.shape[0] * 512
    own_rows = select.shape[1]
    return call(
        queries_kernel,
        count // tile,
        [
            rows(tile, width), column((width, width), 0), full((1, width)), full(table.shape),
            full((width, own_rows)),
        ],
        [
            (rows(tile, wide), (count, wide), BF16),
            (rows(tile, width), (count, width), BF16),
            (rows(tile, own_rows), (count, own_rows), BF16),
        ],
        [],
        6e9,
    )(flags, tokens, weight, bias, table, select)


def run_middle(
    tile, flags, tokens, cotangent, slots, phi, moments, small, query_out, up_own, up_here, up_there,
    down_own, down_here, down_there, bias_own, bias_other, vectors,
):
    count, width = tokens.shape
    half = up_own.shape[1]
    wide = phi.shape[1]
    pairs = width // 128
    return call(
        middle_kernel,
        count // tile,
        [rows(tile, width), rows(tile, width), rows(tile, 128), rows(tile, wide)]
        + table_ins(width)
        + [
            column((width, width), 1),
            full((width, half)),
            pl.BlockSpec(memory_space=pl.ANY),
            pl.BlockSpec(memory_space=pl.ANY),
            full((half, width)),
            pl.BlockSpec(memory_space=pl.ANY),
            pl.BlockSpec(memory_space=pl.ANY),
            full((1, half)),
            full((1, half)),
            full((8, width)),
        ],
        [
            (rows(tile, width), (count, width), BF16),
            (rows(tile, width), (count, width), F32),
            (rows(tile, width), (count, width), F32),
            (rows(tile, 128), (count, 128), F32),
            (rows(tile, width), (count, width), BF16),
            (rows(tile, width), (count, width), F32),
            (rows(tile, half), (count, half), BF16),
            (rows(tile, half), (count, half), BF16),
            (rows(tile, width), (count, width), BF16),
            (rows(tile, width), (count, width), BF16),
            (held((24, width)), (24, width), F32),
            (held((8, half)), (8, half), F32),
        ],
        [
            table_scratch(width),
            pltpu.VMEM((tile, pairs * 256), F32),
            pltpu.VMEM((tile, 2 * half), F32),
            pltpu.VMEM((tile, half), BF16),
            pltpu.VMEM((width, half), BF16),
            pltpu.VMEM((half, width), BF16),
            small_scratch(width),
            pltpu.SemaphoreType.DMA((SLOTS - 1,)),
            pltpu.SemaphoreType.DMA((4,)),
        ],
        30e9,
    )(
        flags, tokens, cotangent, slots, phi, moments, small, query_out, up_own, up_here, up_there,
        down_own, down_here, down_there, bias_own, bias_other, vectors,
    )


def run_attention_back(
    tile, flags, hidden_grad, normed, inverse, att, invden, phi, slots, query_out, gain, select, sums, up_sum
):
    count, width = att.shape
    wide = phi.shape[1]
    pairs = width // 128
    own_rows = select.shape[1]
    half = up_sum.shape[1]
    return call(
        attention_back_kernel,
        count // tile,
        [
            rows(tile, width), rows(tile, width), rows(tile, 128), rows(tile, width), rows(tile, width),
            rows(tile, wide), rows(tile, 128), column((width, width), 1), full((1, width)), full((width, own_rows)),
            full((24, width)), full((8, half)),
        ],
        [
            (rows(tile, width), (count, width), F32),
            (rows(tile, width), (count, width), BF16),
            (rows(tile, 2 * width), (count, 2 * width), BF16),
            (rows(tile, own_rows), (count, own_rows), BF16),
            (held((24, width)), (24, width), F32),
        ]
        + table_outs(width, EXTRA),
        [
            pltpu.VMEM((pairs, 256, 512), F32),
            pltpu.VMEM((SLOTS - 1, pairs, 256, 512), F32),
            small_scratch(width),
            pltpu.SemaphoreType.DMA((SLOTS - 1,)),
        ],
        6e9,
    )(
        flags, hidden_grad, normed, inverse, att, invden, phi, slots, query_out, gain, select, sums, up_sum
    )


def run_queries_back(tile, flags, mixed, phi, scaled, slots, moments, small, table, weight, dfirst):
    count, width = scaled.shape
    wide = phi.shape[1]
    return call(
        queries_back_kernel,
        count // tile,
        [rows(tile, 2 * width), rows(tile, wide), rows(tile, width), rows(tile, 128)]
        + table_ins(width)
        + [full(table.shape), column((width, width), 0), rows(tile, width)],
        [
            (rows(tile, width), (count, width), BF16),
            (rows(tile, width), (count, width), F32),
            (held((8, width)), (8, width), F32),
        ],
        [table_scratch(width), small_scratch(width), pltpu.SemaphoreType.DMA((SLOTS - 1,))],
        8e9,
    )(flags, mixed, phi, scaled, slots, moments, small, table, weight, dfirst)


def run_keys_back(
    tile, flags, phi, values, scaled, slots, moments, small, table, key_weight, value_weight, partial
):
    count, width = scaled.shape
    wide = phi.shape[1]
    return call(
        keys_back_kernel,
        count // tile,
        [rows(tile, wide), rows(tile, width), rows(tile, width), rows(tile, 128)]
        + table_ins(width)
        + [full(table.shape), full(key_weight.shape), full((width, width)), rows(tile, width)],
        [
            (rows(tile, 2 * width), (count, 2 * width), BF16),
            (rows(tile, width), (count, width), BF16),
            (held((8, 2 * width)), (8, 2 * width), F32),
        ],
        [
            table_scratch(width),
            small_scratch(width),
            pltpu.SemaphoreType.DMA((SLOTS - 1,)),
        ],
        12e9,
    )(
        flags, phi, values, scaled, slots, moments, small, table, key_weight, value_weight, partial,
    )


def local(
    tokens, document_lengths, feature_maps, joint_weight, joint_bias, output_weight, output_bias,
    first_gain, first_shift, up_weight, up_bias, down_weight, down_bias, second_gain, second_shift,
    cotangent,
):
    count, width = tokens.shape
    heads, head_size, feature_count = feature_maps.shape
    pairs = heads // 2
    half = up_weight.shape[1]
    tile = TILE
    tiles = count // tile
    rank = lax.axis_index("dp")
    dp = lax.axis_size("dp")
    mp = lax.axis_size("mp")
    mp_rank = lax.axis_index("mp")

    lengths = document_lengths[0]
    ends = jnp.cumsum(lengths)
    place = rank * count + jnp.arange(count, dtype=jnp.int32)
    document = jnp.sum((ends[None, :] <= place[:, None]).astype(jnp.int32), axis=1)
    longest = jnp.argmax(lengths).astype(jnp.int32)
    slot = jnp.where(
        document == longest,
        0,
        jnp.where(document >= SLOTS, SLOTS, jnp.where(document < longest, document + 1, document)),
    )
    slots = jnp.broadcast_to(slot[:, None], (count, 128))
    order = jnp.arange(SLOTS, dtype=jnp.int32)
    which = jnp.where(order - 1 < longest, order - 1, order)
    starts = jnp.where(which > 0, ends[jnp.maximum(which - 1, 0)], 0)
    stops = ends[jnp.maximum(which, 0)]
    base = rank * count + jnp.arange(tiles, dtype=jnp.int32)[:, None] * tile
    all_main = jnp.max(slot.reshape(tiles, tile), axis=1, keepdims=True) == 0
    starts_in = jnp.clip(starts[None, :] - base, 0, tile)
    stops_in = jnp.clip(stops[None, :] - base, 0, tile)
    present = jnp.max((stops_in > starts_in).astype(jnp.int32), axis=0, keepdims=True)
    flags = jnp.concatenate(
        [
            all_main.astype(jnp.int32),
            starts_in[:, 1:],
            stops_in,
            jnp.broadcast_to(present, (tiles, SLOTS)),
            jnp.broadcast_to(mine(1).astype(jnp.int32), (tiles, SLOTS)),
        ],
        axis=1,
    )

    shard = joint_weight.shape[0]
    small_vectors = jnp.concatenate(
        [joint_bias, output_bias, first_gain, first_shift, second_gain, second_shift]
    )
    vector_size = small_vectors.shape[0]
    lines = -(-vector_size // 128)
    small_vectors = jnp.pad(small_vectors, (0, lines * 128 - vector_size)).reshape(lines, 128)
    small_vectors = jnp.pad(small_vectors, ((0, shard - lines), (0, 0)))
    shards = jnp.concatenate([joint_weight[:, width:], small_vectors], axis=1)
    query_out = lax.all_gather(
        jnp.concatenate([joint_weight[:, :width], output_weight], axis=1), ("dp", "mp"), axis=0, tiled=True
    )
    shards = join_pair(shards, swap_mp(shards), mp_rank, 0).reshape(2 * shard, -1)
    key_chain = Gather(
        jnp.concatenate([shards[:, :width], shards[:, 2 * width :]], axis=1), far_first()
    )
    value_chain = Gather(shards[:, width : 2 * width], near_first())

    core = mine(1)

    def own_part(a):
        return lax.dynamic_slice_in_dim(a, core * (a.shape[0] // 2), a.shape[0] // 2, 0)

    while key_chain.order:
        key_chain.start()
        value_chain.start()
        if len(key_chain.order) == len(dp_bits()):
            up_here = swap_mp(after(own_part(up_weight), shards))
            down_here = swap_mp(after(own_part(down_weight), up_here))
        key_chain.finish()
        value_chain.finish()
    key_weight = key_chain.result()
    value_weight = value_chain.result()

    vectors_all = key_weight[:, width:].reshape(dp * mp, shard, 128)[:, :lines].reshape(dp * mp, -1)
    bias_part = joint_bias.shape[0]
    joint_offset = vectors_all[:, :bias_part].reshape(1, -1).astype(F32)
    bias_own = up_bias[None, :].astype(F32)

    pair_maps = feature_maps.reshape(pairs, 2, head_size, feature_count)
    blank = jnp.zeros_like(pair_maps[:, 0])
    table = jnp.concatenate(
        [
            jnp.concatenate([pair_maps[:, 0], blank], axis=2),
            jnp.concatenate([blank, pair_maps[:, 1]], axis=2),
            jnp.concatenate([blank + 1, blank], axis=2),
            jnp.concatenate([blank, blank + 1], axis=2),
        ],
        axis=1,
    )
    own_rows = width // mp
    index = jnp.arange(own_rows, dtype=jnp.int32)
    source = index // shard * (shard * mp) + mp_rank * shard + index % shard
    select = (jnp.arange(width, dtype=jnp.int32)[:, None] == source[None, :]).astype(BF16)

    phi_k, values, scaled_k, moments, small_moments = run_keys(
        TILE, flags, tokens, key_weight, value_weight, joint_offset[:, width:], table, slots
    )

    up_there = swap_dp(after(up_here, moments), 1)
    down_there = swap_dp(after(down_here, up_there), 1)
    bias_other = swap_mp(after(up_bias, moments)[None, :]).astype(F32)
    vectors_all = after(vectors_all, moments)
    parts = [
        vectors_all[:, bias_part + i * shard : bias_part + (i + 1) * shard].reshape(-1).astype(F32)
        for i in range(5)
    ]
    vectors = jnp.stack(
        [parts[0], parts[1], parts[2], down_bias.astype(F32), parts[3], parts[4], parts[4], parts[4]]
    )
    bits = dp_bits()
    far, others = bits[0], bits[1:-1]
    moments_sum = TableSum(moments).add()
    for bit in reversed(others):
        moments_sum.swap(bit).add()
    moments_sum.swap(far)
    phi_q, scaled_q, tokens_own = run_queries(
        TILE, flags, after(tokens, moments_sum.own), query_out, joint_offset[:, :width], table, select
    )
    moments = moments_sum.add(phi_q).swap(1).join()
    (
        layer_output, hidden_grad, normed, inverse, att, invden, active, dup, hidden_low, dffn, sums, up_sum,
    ) = run_middle(
        TILE, flags, tokens, cotangent, slots, phi_q, moments, small_moments, query_out, up_weight,
        up_here, up_there, down_weight, down_here, down_there, bias_own, bias_other, vectors,
    )

    near = others[-1:]
    middle_bits = others[:-1]
    down_order = [1] + near + middle_bits
    up_order = [1] + middle_bits + near
    down_grad = tn(active, dffn).astype(BF16)
    down = Scatter(down_grad, down_order).start()
    up_grad = tn(after(hidden_low, down_grad), dup).astype(BF16)
    down.finish(up_grad)
    up = Scatter(up_grad, up_order).start(down.a)
    down.start()
    up.finish(down.a).start()

    dfirst, dbranch, mixed, att_own, first_sums, dmoments, small_dmoments = run_attention_back(
        TILE, flags, after(hidden_grad, up.a, down.a), normed, inverse, att, invden, phi_q, slots,
        query_out, vectors[1:2], select, sums, up_sum,
    )

    dmoments_sum = TableSum(dmoments)
    down.finish(dmoments)
    up.finish(down.a)
    dmoments_sum.add(up.a)
    for place, bit in enumerate(middle_bits):
        dmoments_sum.swap(bit)
        if place == 0:
            down.start(dmoments_sum.own)
            up.start(dmoments_sum.own)
            out_grad = tn(after(att_own, dmoments_sum.own), dbranch).astype(BF16)
            dmoments_sum.add(out_grad)
        else:
            dmoments_sum.add()
    dmoments_sum.swap(far)
    dquery, partial_tokens, query_sums = run_queries_back(
        TILE, flags, mixed, phi_q, scaled_q, slots, moments, small_moments, table, query_out,
        after(dfirst, dmoments_sum.own),
    )
    dmoments_sum.add(dquery).swap(near[0])
    down.finish(dmoments_sum.own)
    up.finish(down.a)
    while down.order:
        down.start().finish()
        up.start().finish()
    down.start_swap()
    up.start_swap(down.a)
    query_grad = tn(after(tokens_own, dmoments_sum.own), dquery).astype(BF16)
    query_out_grad = Scatter(jnp.concatenate([query_grad, out_grad], axis=1), down_order + [far])
    query_out_grad.start(dmoments_sum.add(query_grad).own)
    dmoments_sum.swap(1)
    query_out_grad.finish(dmoments_sum.own).start()
    dmoments = dmoments_sum.join(query_out_grad.a)
    dkey_value, tokens_grad, key_sums = run_keys_back(
        TILE, flags, phi_k, values, scaled_k, slots, dmoments, small_dmoments, table, key_weight,
        value_weight, after(partial_tokens, query_out_grad.a),
    )
    key_value_grad = tn(tokens_own, dkey_value).astype(BF16)
    biases = jnp.concatenate([jnp.sum(query_sums, axis=0), jnp.sum(key_sums, axis=0)])
    biases = biases.reshape(dp * shard, -1)
    bias_columns = biases.shape[1]
    biases = jnp.pad(biases, ((0, 0), (0, 128 - bias_columns))).astype(BF16)
    key_value_sum = Scatter(jnp.concatenate([key_value_grad, biases], axis=1), up_order + [far]).start()

    down.finish_swap(dkey_value)
    up.finish_swap(down.a)
    down = down.gather(middle_bits[::-1] + near + [1]).start()
    up = up.gather(near + middle_bits[::-1] + [1]).start()
    key_value_sum.finish(up.a, down.a).start()
    query_out_grad.finish(key_value_sum.a).start()
    down.finish(query_out_grad.a).start()
    up.finish(down.a).start()
    key_value_sum.finish(up.a)
    query_out_grad.finish(key_value_sum.a)
    while down.order:
        if key_value_sum.order:
            key_value_sum.start()
        if query_out_grad.order:
            query_out_grad.start()
        down.finish(key_value_sum.a)
        up.finish(down.a)
        if down.order:
            down.start()
            up.start()
        if query_out_grad.got is not None and query_out_grad.order:
            query_out_grad.finish(up.a)
        if key_value_sum.order:
            key_value_sum.finish(up.a)
    down_total = down.result()
    up_total = up.result()
    query_out_total = query_out_grad.rest().astype(F32)
    key_value_total = key_value_sum.rest().astype(F32)

    extra = dmoments[width + 16 :].reshape(-1).astype(F32)

    def owned(place, size=width):
        part = size // (dp * mp)
        start = place * width + (rank * mp + mp_rank) * part
        return lax.dynamic_slice_in_dim(extra, start, part, 0)

    bias_total = key_value_total[:, 2 * width : 2 * width + bias_columns].reshape(mp, -1)
    bias_total = lax.dynamic_index_in_dim(bias_total, mp_rank, 0, False)

    return (
        layer_output,
        tokens_grad,
        jnp.concatenate([query_out_total[:, :width], key_value_total[:, : 2 * width]], axis=1),
        bias_total,
        query_out_total[:, width:],
        owned(2),
        owned(0),
        owned(1),
        up_total.astype(F32),
        extra[6 * width : 6 * width + half],
        down_total.astype(F32),
        extra[5 * width : 6 * width],
        owned(3),
        owned(4),
    )


def solution(mesh):
    shared = P(("dp", "mp"))
    in_specs = (
        P("dp", None), P(), P(), P(("dp", "mp"), None), shared, P(("dp", "mp"), None), shared, shared,
        shared, P(None, "mp"), P("mp"), P("mp", None), P(), shared, shared, P("dp", None),
    )
    out_specs = (
        P("dp", None), P("dp", None), P(("dp", "mp"), None), shared, P(("dp", "mp"), None), shared,
        shared, shared, P(None, "mp"), P("mp"), P("mp", None), P(), shared, shared,
    )
    return jax.shard_map(local, mesh=mesh, in_specs=in_specs, out_specs=out_specs, check_vma=False)
```

profile of v0, /device:TPU:0, one launch (start us, length us, event | category | flops | bytes accessed | tf_op | source)
XLA Modules:
  0.0 330.2 jit_solution(17013590330985141040)
XLA Ops:
  7.2 4.1 %concatenate.296 = bf16[192]{0:T(256)(128)(2,1)S(1)} concatenate(bf16[72]{0:T(256)(128)(2,1)} %param.20, bf16[24]{0:T(256)(128)(2,1)} %param.22, bf16[24]{0:T(256)(128)(2,1)} %param.23, bf16[24]{0:T(256)(128)(2,1)} %param.24, bf16[24]{0:T(256)(128)(2,1)} %param.29, bf16[24]{0:T(256)(128)(2,1)} %param.30), dimensions={0} | concatenate | bytes 768 | tf_op jit(solution)/shard_map/concatenate | solution.py:938
  12.3 3.0 collective-permute-start
  30.7 2.7 collective-permute-start.1
  34.0 2.3 collective-permute-start.6
  36.3 5.8 %collective-permute-done.1 = bf16[48,896]{1,0:T(8,128)(2,1)S(1)} collective-permute-done((bf16[48,896]{1,0:T(8,128)(2,1)S(1)}, bf16[48,896]{1,0:T(8,128)(2,1)S(1)}, u32[]{:S(2)}, u32[]{:S(2)}) %collective-permute-start.1) | collective-permute-done | bytes 86048 | tf_op jit(solution)/shard_map/ppermute | solution.py:65
  42.4 2.3 collective-permute-done.6
  44.9 5.7 %collective-permute-done.2 = bf16[2,48,896]{2,1,0:T(8,128)(2,1)S(1)} collective-permute-done((bf16[2,48,896]{2,1,0:T(8,128)(2,1)S(1)}, bf16[2,48,896]{2,1,0:T(8,128)(2,1)S(1)}, u32[]{:S(2)}, u32[]{:S(2)}) %collective-permute-start.2) | collective-permute-done | bytes 172064 | tf_op jit(solution)/shard_map/ppermute | solution.py:65
  50.8 6.5 %collective-permute-done.7 = bf16[2,2,48,768]{3,2,1,0:T(8,128)(2,1)S(1)} collective-permute-done((bf16[2,2,48,768]{3,2,1,0:T(8,128)(2,1)S(1)}, bf16[2,2,48,768]{3,2,1,0:T(8,128)(2,1)S(1)}, u32[]{:S(2)}, u32[]{:S(2)}) %collective-permute-start.7) | collective-permute-done | bytes 294944 | tf_op jit(solution)/shard_map/ppermute | solution.py:65
  65.3 15.7 %shard_map.263 = (bf16[1024,3072]{1,0:T(8,128)(2,1)}, bf16[1024,768]{1,0:T(8,128)(2,1)}, bf16[1024,768]{1,0:T(8,128)(2,1)}, bf16[784,256]{1,0:T(8,128)(2,1)}, bf16[5488,256]{1,0:T(8,128)(2,1)}) custom-call(s32[4,32]{1,0:T(4,128)} %concatenate.295.flags, bf16[1024,768]{1,0:T(8,128)(2,1)} %x.18, bf16[768,896]{1,0:T(8,128)(2,1)} %bitcast.220, ...), custom_call_target="tpu_custom_call" | custom-call | flops 10000000000 | bytes 20000000 | tf_op jit(solution)/shard_map/pallas_call | solution.py:705
  85.9 6.4 %collective-permute-done.10 = bf16[392,256]{1,0:T(8,128)(2,1)S(1)} collective-permute-done((bf16[392,256]{1,0:T(8,128)(2,1)S(1)}, bf16[392,256]{1,0:T(8,128)(2,1)S(1)}, u32[]{:S(2)}, u32[]{:S(2)}) %collective-permute-start.10) | collective-permute-done | bytes 200736 | tf_op jit(solution)/shard_map/ppermute | solution.py:65
  95.5 3.2 collective-permute-done.11
  100.4 8.8 %shard_map.264 = (bf16[1024,3072]{1,0:T(8,128)(2,1)}, bf16[1024,768]{1,0:T(8,128)(2,1)}, bf16[1024,384]{1,0:T(8,128)(2,1)}) custom-call(s32[4,32]{1,0:T(4,128)} %concatenate.295.flags, bf16[1024,768]{1,0:T(8,128)(2,1)} %x.18, bf16[768,1536]{1,0:T(8,128)(2,1)} %all-gather.2.cloned.1.call-done.weight.out_weight, f32[1,768]{1,0:T(1,128)} %slice.121.bias, ...), custom_call_target="tpu_custom_call" | custom-call | flops 6000000000 | bytes 20000000 | tf_op jit(solution)/shard_map/pallas_call | solution.py:734
  112.2 40.8 %shard_map.265 = (bf16[1024,768]{1,0:T(8,128)(2,1)}, f32[1024,768]{1,0:T(8,128)}, f32[1024,768]{1,0:T(8,128)}, f32[1024,128]{1,0:T(8,128)}, bf16[1024,768]{1,0:T...) custom-call(s32[4,32]{1,0:T(4,128)} %concatenate.295.flags, ...), custom_call_target="tpu_custom_call" | custom-call | flops 30000001024 | bytes 20000000 | tf_op jit(solution)/shard_map/pallas_call | solution.py:759
  153.1 5.2 %convolution_convert_fusion.1 = bf16[1536,768]{1,0:T(8,128)(2,1)S(1)} fusion(bf16[1024,1536]{1,0:T(8,128)(2,1)} %get-tuple-element.109, bf16[1024,768]{1,0:T(8,128)(2,1)} %get-tuple-element.110), kind=kOutput, calls=%fused_computation.5 | convolution fusion | flops 2417098752 | bytes 7077888 | tf_op jit(solution)/shard_map/dot_general | solution.py:31
  159.7 3.2 convolution_convert_fusion
  164.4 3.1 collective-permute-done.20
  169.2 18.9 %shard_map.266 = (f32[1024,768]{1,0:T(8,128)}, bf16[1024,768]{1,0:T(8,128)(2,1)}, bf16[1024,1536]{1,0:T(8,128)(2,1)}, bf16[1024,384]{1,0:T(8,128)(2,1)}, f32[24,...) custom-call(s32[4,32]{1,0:T(4,128)} %concatenate.295.flags, ...), custom_call_target="tpu_custom_call" | custom-call | flops 6000000000 | bytes 20000000 | tf_op jit(solution)/shard_map/pallas_call | solution.py:816
  195.1 3.7 %collective-permute-done.24 = bf16[408,256]{1,0:T(8,128)(2,1)S(1)} collective-permute-done((bf16[408,256]{1,0:T(8,128)(2,1)S(1)}, bf16[408,256]{1,0:T(8,128)(2,1)S(1)}, u32[]{:S(2)}, u32[]{:S(2)}) %collective-permute-start.24) | collective-permute-done | bytes 208928 | tf_op jit(solution)/shard_map/ppermute | solution.py:65
  198.8 4.3 %collective-permute-start.25 = (bf16[408,256]{1,0:T(8,128)(2,1)S(1)}, bf16[408,256]{1,0:T(8,128)(2,1)}, u32[]{:S(2)}, u32[]{:S(2)}) collective-permute-start(bf16[408,256]{1,0:T(8,128)(2,1)S(1)} %add_convert_fusion.4), channel_id=1, source_target_pairs={{0,16},{2,18},{4,20},{6,22},{8,24},{10,26},{12,28},{14,30},{16,0},... | collective-permute-start | bytes 626696 | tf_op jit(solution)/shard_map/ppermute | solution.py:65
  203.1 17.1 %shard_map.267 = (bf16[1024,768]{1,0:T(8,128)(2,1)}, f32[1024,768]{1,0:T(8,128)}, f32[8,768]{1,0:T(8,128)}) custom-call(s32[4,32]{1,0:T(4,128)} %concatenate.295.flags, bf16[1024,1536]{1,0:T(8,128)(2,1)} %get-tuple-element.131.mixed, bf16[1024,3072]{1,0:T(8,128)(2,1)} %get-tuple-element.94.phi, bf16[1024,768]{1,0:T(8,128)(2,1)} %get-tuple-element.132.scaled, ...), custom_call_target="tpu_custom_call" | custom-call | flops 8000000000 | bytes 20000000 | tf_op jit(solution)/shard_map/pallas_call | solution.py:847
  222.1 2.2 convolution_convert_fusion.3
  224.5 3.4 %collective-permute-done.26 = bf16[408,256]{1,0:T(8,128)(2,1)S(1)} collective-permute-done((bf16[408,256]{1,0:T(8,128)(2,1)S(1)}, bf16[408,256]{1,0:T(8,128)(2,1)S(1)}, u32[]{:S(2)}, u32[]{:S(2)}) %collective-permute-start.26) | collective-permute-done | bytes 208928 | tf_op jit(solution)/shard_map/ppermute | solution.py:65
  228.4 3.0 collective-permute-start.33
  233.6 20.8 %shard_map.268 = (bf16[1024,1536]{1,0:T(8,128)(2,1)}, bf16[1024,768]{1,0:T(8,128)(2,1)}, f32[8,1536]{1,0:T(8,128)}) custom-call(s32[4,32]{1,0:T(4,128)} %concatenate.295.flags, bf16[1024,3072]{1,0:T(8,128)(2,1)} %get-tuple-element.104.phi, bf16[1024,768]{1,0:T(8,128)(2,1)} %get-tuple-element.105.values, bf16[1024,768]{1,0:T(8,128)(2,1)} %get-tuple-element.106.scaled, ...), custom_call_target="tpu_custom_call" | custom-call | flops 12000000000 | bytes 20000000 | tf_op jit(solution)/shard_map/pallas_call | solution.py:868
  255.5 3.3 convolution_convert_fusion.2
  269.1 7.8 %collective-permute-done.29 = bf16[2,2,24,1536]{3,2,0,1:T(8,128)(2,1)S(1)} collective-permute-done((bf16[2,2,24,1536]{3,2,0,1:T(8,128)(2,1)}, bf16[2,2,24,1536]{3,2,0,1:T(8,128)(2,1)S(1)}, u32[]{:S(2)}, u32[]{:S(2)}) %collective-permute-start.29) | collective-permute-done | bytes 294944 | tf_op jit(solution)/shard_map/ppermute | solution.py:65
  281.9 13.7 %collective-permute-done.35 = bf16[2,24,1536]{2,1,0:T(8,128)(2,1)S(1)} collective-permute-done((bf16[2,24,1536]{2,1,0:T(8,128)(2,1)S(1)}, bf16[2,24,1536]{2,1,0:T(8,128)(2,1)S(1)}, u32[]{:S(2)}, u32[]{:S(2)}) %collective-permute-start.35) | collective-permute-done | bytes 147488 | tf_op jit(solution)/shard_map/ppermute | solution.py:65
  295.7 6.8 %collective-permute-start.39 = (bf16[24,1536]{1,0:T(8,128)(2,1)S(1)}, bf16[24,1536]{1,0:T(8,128)(2,1)S(1)}, u32[]{:S(2)}, u32[]{:S(2)}) collective-permute-start(bf16[24,1536]{1,0:T(8,128)(2,1)S(1)} %dynamic-slice_bitcast_fusion.13), channel_id=1, source_target_pairs={{0,16},{2,18},{4,20},{6,22},{8,24},{10,26},{12,28},{14,30},{16,0},... | collective-permute-start | bytes 221192 | tf_op jit(solution)/shard_map/ppermute | solution.py:65
  306.7 5.5 %collective-permute-done.43 = bf16[24,1664]{1,0:T(8,128)(2,1)S(1)} collective-permute-done((bf16[24,1664]{1,0:T(8,128)(2,1)S(1)}, bf16[24,1664]{1,0:T(8,128)(2,1)S(1)}, u32[]{:S(2)}, u32[]{:S(2)}) %collective-permute-start.43) | collective-permute-done | bytes 79904 | tf_op jit(solution)/shard_map/ppermute | solution.py:65
  315.2 2.1 fusion.4
  317.3 2.6 copy.68
  320.3 2.6 copy.69
  (253 shorter events, 77.9 us)
Async XLA Ops:
  7.2 93.2 %all-gather.2.cloned.1.call-start = ((), (), s32[]{:S(2)}) async-start(), calls=%async_computation | async-start | bytes 2433024 | tf_op jit(solution)/shard_map/all_gather | solution.py:946
  12.3 16.7 %collective-permute-start = (bf16[24,1664]{1,0:T(8,128)(2,1)S(1)}, bf16[24,1664]{1,0:T(8,128)(2,1)S(1)}, u32[]{:S(2)}, u32[]{:S(2)}) collective-permute-start(bf16[24,1664]{1,0:T(8,128)(2,1)S(1)} %get-tuple-element.188), channel_id=1, source_target_pairs={{0,1},{1,0},{2,3},{3,2},{4,5},{5,4},{6,7},{7,6},{8,9},{9,8},{10,11... | collective-permute-start | bytes 239624 | tf_op jit(solution)/shard_map/ppermute | solution.py:69
  30.7 11.4 %collective-permute-start.1 = (bf16[48,896]{1,0:T(8,128)(2,1)S(1)}, bf16[48,896]{1,0:T(8,128)(2,1)S(1)}, u32[]{:S(2)}, u32[]{:S(2)}) collective-permute-start(bf16[48,896]{1,0:T(8,128)(2,1)S(1)} %get-tuple-element.186), channel_id=1, source_target_pairs={{0,16},{2,18},{4,20},{6,22},{8,24},{10,26},{12,28},{14,30},{16,0},... | collective-permute-start | bytes 258056 | tf_op jit(solution)/shard_map/ppermute | solution.py:65
  33.4 29.1 %collective-permute-start.14 = (bf16[384,1536]{1,0:T(8,128)(2,1)S(1)}, bf16[384,1536]{1,0:T(8,128)(2,1)}, u32[]{:S(2)}, u32[]{:S(2)}) collective-permute-start(bf16[384,1536]{1,0:T(8,128)(2,1)S(1)} %constant_dynamic-slice_fusion.5), channel_id=1, source_target_pairs={{0,1},{1,0},{2,3},{3,2},{4,5},{5,4},{6,7},{7,6},{8,9},{9,8},{10,11... | collective-permute-start | bytes 3538952 | tf_op jit(solution)/shard_map/ppermute | solution.py:69
  34.0 10.7 %collective-permute-start.6 = (bf16[2,48,768]{2,1,0:T(8,128)(2,1)S(1)}, bf16[2,48,768]{2,1,0:T(8,128)(2,1)S(1)}, u32[]{:S(2)}, u32[]{:S(2)}) collective-permute-start(bf16[2,48,768]{2,1,0:T(8,128)(2,1)S(1)} %maximum_select_fusion.25), channel_id=1, source_target_pairs={{0,16},{2,18},{4,20},{6,22},{8,24},{10,26},{12,28},{14,30},{16,0},... | collective-permute-start | bytes 442376 | tf_op jit(solution)/shard_map/ppermute | solution.py:65
  42.1 8.4 %collective-permute-start.2 = (bf16[2,48,896]{2,1,0:T(8,128)(2,1)S(1)}, bf16[2,48,896]{2,1,0:T(8,128)(2,1)S(1)}, u32[]{:S(2)}, u32[]{:S(2)}) collective-permute-start(bf16[2,48,896]{2,1,0:T(8,128)(2,1)S(1)} %maximum_select_fusion.22), channel_id=1, source_target_pairs={{0,8},{2,10},{4,12},{6,14},{8,0},{10,2},{12,4},{14,6},{16,24},{18,... | collective-permute-start | bytes 516104 | tf_op jit(solution)/shard_map/ppermute | solution.py:65
  44.7 12.6 %collective-permute-start.7 = (bf16[2,2,48,768]{3,2,1,0:T(8,128)(2,1)S(1)}, bf16[2,2,48,768]{3,2,1,0:T(8,128)(2,1)S(1)}, u32[]{:S(2)}, u32[]{:S(2)}) collective-permute-start(bf16[2,2,48,768]{3,2,1,0:T(8,128)(2,1)S(1)} %maximum_select_fusion.20), channel_id=1, source_target_pairs={{0,8},{2,10},{4,12},{6,14},{8,0},{10,2},{12,4},{14,6},{16,24},{18,... | collective-permute-start | bytes 884744 | tf_op jit(solution)/shard_map/ppermute | solution.py:65
  50.6 7.3 %collective-permute-start.3 = (bf16[2,2,48,896]{3,2,0,1:T(8,128)(2,1)S(1)}, bf16[2,2,48,896]{3,2,0,1:T(8,128)(2,1)S(1)}, u32[]{:S(2)}, u32[]{:S(2)}) collective-permute-start(bf16[2,2,48,896]{3,2,0,1:T(8,128)(2,1)S(1)} %maximum_select_fusion.18), channel_id=1, source_target_pairs={{0,4},{2,6},{4,0},{6,2},{8,12},{10,14},{12,8},{14,10},{16,20},{18,... | collective-permute-start | bytes 1032200 | tf_op jit(solution)/shard_map/ppermute | solution.py:65
  62.5 33.1 %collective-permute-start.16 = (bf16[768,768]{1,0:T(8,128)(2,1)S(1)}, bf16[768,768]{1,0:T(8,128)(2,1)}, u32[]{:S(2)}, u32[]{:S(2)}) collective-permute-start(bf16[768,768]{1,0:T(8,128)(2,1)S(1)} %constant_dynamic-slice_fusion.4), channel_id=1, source_target_pairs={{0,1},{1,0},{2,3},{3,2},{4,5},{5,4},{6,7},{7,6},{8,9},{9,8},{10,11... | collective-permute-start | bytes 3538952 | tf_op jit(solution)/shard_map/ppermute | solution.py:69
  81.0 14.5 %collective-permute-start.15 = (bf16[384,1536]{1,0:T(8,128)(2,1)}, bf16[384,1536]{1,0:T(8,128)(2,1)}, u32[]{:S(2)}, u32[]{:S(2)}) collective-permute-start(bf16[384,1536]{1,0:T(8,128)(2,1)} %collective-permute-done.14.up_here), channel_id=1, source_target_pairs={{0,2},{2,0},{4,6},{6,4},{8,10},{10,8},{12,14},{14,12},{16,18},{18,... | collective-permute-start | bytes 3538952 | tf_op jit(solution)/shard_map/ppermute | solution.py:65
  94.0 16.8 %collective-permute-start.18 = (bf16[1,1536]{1,0:T(2,128)(2,1)S(1)}, bf16[1,1536]{1,0:T(2,128)(2,1)S(1)}, u32[]{:S(2)}, u32[]{:S(2)}) collective-permute-start(bf16[1,1536]{1,0:T(2,128)(2,1)S(1)} %broadcast_in_dim.25), channel_id=1, source_target_pairs={{0,1},{1,0},{2,3},{3,2},{4,5},{5,4},{6,7},{7,6},{8,9},{9,8},{10,11... | collective-permute-start | bytes 9224 | tf_op jit(solution)/shard_map/ppermute | solution.py:69
  95.5 16.7 %collective-permute-start.17 = (bf16[768,768]{1,0:T(8,128)(2,1)}, bf16[768,768]{1,0:T(8,128)(2,1)}, u32[]{:S(2)}, u32[]{:S(2)}) collective-permute-start(bf16[768,768]{1,0:T(8,128)(2,1)} %collective-permute-done.16.down_here), channel_id=1, source_target_pairs={{0,2},{2,0},{4,6},{6,4},{8,10},{10,8},{12,14},{14,12},{16,18},{18,... | collective-permute-start | bytes 3538952 | tf_op jit(solution)/shard_map/ppermute | solution.py:65
  98.8 10.7 %collective-permute-start.12 = (bf16[392,256]{1,0:T(8,128)(2,1)S(1)}, bf16[392,256]{1,0:T(8,128)(2,1)S(1)}, u32[]{:S(2)}, u32[]{:S(2)}) collective-permute-start(bf16[392,256]{1,0:T(8,128)(2,1)S(1)} %add_convert_fusion.6), channel_id=1, source_target_pairs={{0,16},{2,18},{4,20},{6,22},{8,24},{10,26},{12,28},{14,30},{16,0},... | collective-permute-start | bytes 602120 | tf_op jit(solution)/shard_map/ppermute | solution.py:65
  164.4 24.8 %collective-permute-start.23 = (bf16[2,2,96,768]{3,2,1,0:T(8,128)(2,1)S(1)}, bf16[2,2,96,768]{3,2,1,0:T(8,128)(2,1)S(1)}, u32[]{:S(2)}, u32[]{:S(2)}) collective-permute-start(bf16[2,2,96,768]{3,2,1,0:T(8,128)(2,1)S(1)} %dynamic-slice_bitcast_fusion.2), channel_id=1, source_target_pairs={{0,4},{2,6},{4,0},{6,2},{8,12},{10,14},{12,8},{14,10},{16,20},{18,... | collective-permute-start | bytes 1769480 | tf_op jit(solution)/shard_map/ppermute | solution.py:65
  169.1 20.2 %collective-permute-start.22 = (bf16[2,2,48,1536]{3,2,1,0:T(8,128)(2,1)S(1)}, bf16[2,2,48,1536]{3,2,1,0:T(8,128)(2,1)S(1)}, u32[]{:S(2)}, u32[]{:S(2)}) collective-permute-start(bf16[2,2,48,1536]{3,2,1,0:T(8,128)(2,1)S(1)} %dynamic-slice_bitcast_fusion.3), channel_id=1, source_target_pairs={{0,8},{2,10},{4,12},{6,14},{8,0},{10,2},{12,4},{14,6},{16,24},{18,... | collective-permute-start | bytes 1769480 | tf_op jit(solution)/shard_map/ppermute | solution.py:65
  190.7 8.1 %collective-permute-start.24 = (bf16[408,256]{1,0:T(8,128)(2,1)S(1)}, bf16[408,256]{1,0:T(8,128)(2,1)S(1)}, u32[]{:S(2)}, u32[]{:S(2)}) collective-permute-start(bf16[408,256]{1,0:T(8,128)(2,1)S(1)} %fusion.21), channel_id=1, source_target_pairs={{0,8},{2,10},{4,12},{6,14},{8,0},{10,2},{12,4},{14,6},{16,24},{18,... | collective-permute-start | bytes 626696 | tf_op jit(solution)/shard_map/ppermute | solution.py:65
  191.5 36.7 %collective-permute-start.31 = (bf16[2,48,1536]{2,1,0:T(8,128)(2,1)}, bf16[2,48,1536]{2,1,0:T(8,128)(2,1)S(1)}, u32[]{:S(2)}, u32[]{:S(2)}) collective-permute-start(bf16[2,48,1536]{2,1,0:T(8,128)(2,1)} %dynamic-slice_bitcast_fusion.6), channel_id=1, source_target_pairs={{0,4},{2,6},{4,0},{6,2},{8,12},{10,14},{12,8},{14,10},{16,20},{18,... | collective-permute-start | bytes 884744 | tf_op jit(solution)/shard_map/ppermute | solution.py:65
  192.3 32.1 %collective-permute-start.32 = (bf16[2,96,768]{2,1,0:T(8,128)(2,1)}, bf16[2,96,768]{2,1,0:T(8,128)(2,1)S(1)}, u32[]{:S(2)}, u32[]{:S(2)}) collective-permute-start(bf16[2,96,768]{2,1,0:T(8,128)(2,1)} %dynamic-slice_bitcast_fusion.5), channel_id=1, source_target_pairs={{0,8},{2,10},{4,12},{6,14},{8,0},{10,2},{12,4},{14,6},{16,24},{18,... | collective-permute-start | bytes 884744 | tf_op jit(solution)/shard_map/ppermute | solution.py:65
  198.8 22.2 %collective-permute-start.25 = (bf16[408,256]{1,0:T(8,128)(2,1)S(1)}, bf16[408,256]{1,0:T(8,128)(2,1)}, u32[]{:S(2)}, u32[]{:S(2)}) collective-permute-start(bf16[408,256]{1,0:T(8,128)(2,1)S(1)} %add_convert_fusion.4), channel_id=1, source_target_pairs={{0,16},{2,18},{4,20},{6,22},{8,24},{10,26},{12,28},{14,30},{16,0},... | collective-permute-start | bytes 626696 | tf_op jit(solution)/shard_map/ppermute | solution.py:65
  228.2 31.7 %collective-permute-start.34 = (bf16[2,96,768]{2,1,0:T(8,128)(2,1)S(1)}, bf16[2,96,768]{2,1,0:T(8,128)(2,1)S(1)}, u32[]{:S(2)}, u32[]{:S(2)}) collective-permute-start(bf16[2,96,768]{2,1,0:T(8,128)(2,1)S(1)} %fusion.18), channel_id=1, source_target_pairs={{0,16},{2,18},{4,20},{6,22},{8,24},{10,26},{12,28},{14,30},{16,0},... | collective-permute-start | bytes 884744 | tf_op jit(solution)/shard_map/ppermute | solution.py:65
  228.4 31.7 %collective-permute-start.33 = (bf16[2,48,1536]{2,1,0:T(8,128)(2,1)S(1)}, bf16[2,48,1536]{2,1,0:T(8,128)(2,1)}, u32[]{:S(2)}, u32[]{:S(2)}) collective-permute-start(bf16[2,48,1536]{2,1,0:T(8,128)(2,1)S(1)} %fusion.19), channel_id=1, source_target_pairs={{0,16},{2,18},{4,20},{6,22},{8,24},{10,26},{12,28},{14,30},{16,0},... | collective-permute-start | bytes 884744 | tf_op jit(solution)/shard_map/ppermute | solution.py:65
  260.0 17.0 %collective-permute-start.38 = (bf16[2,96,768]{2,1,0:T(8,128)(2,1)S(1)}, bf16[2,96,768]{2,1,0:T(8,128)(2,1)S(1)}, u32[]{:S(2)}, u32[]{:S(2)}) collective-permute-start(bf16[2,96,768]{2,1,0:T(8,128)(2,1)S(1)} %add_convert_fusion.1), channel_id=1, source_target_pairs={{0,8},{2,10},{4,12},{6,14},{8,0},{10,2},{12,4},{14,6},{16,24},{18,... | collective-permute-start | bytes 884744 | tf_op jit(solution)/shard_map/ppermute | solution.py:65
  261.1 16.3 %collective-permute-start.37 = (bf16[2,48,1536]{2,1,0:T(8,128)(2,1)S(1)}, bf16[2,48,1536]{2,1,0:T(8,128)(2,1)S(1)}, u32[]{:S(2)}, u32[]{:S(2)}) collective-permute-start(bf16[2,48,1536]{2,1,0:T(8,128)(2,1)S(1)} %add_convert_fusion), channel_id=1, source_target_pairs={{0,4},{2,6},{4,0},{6,2},{8,12},{10,14},{12,8},{14,10},{16,20},{18,... | collective-permute-start | bytes 884744 | tf_op jit(solution)/shard_map/ppermute | solution.py:65
  261.9 15.0 %collective-permute-start.29 = (bf16[2,2,24,1536]{3,2,0,1:T(8,128)(2,1)}, bf16[2,2,24,1536]{3,2,0,1:T(8,128)(2,1)S(1)}, u32[]{:S(2)}, u32[]{:S(2)}) collective-permute-start(bf16[2,2,24,1536]{3,2,0,1:T(8,128)(2,1)} %dynamic-slice_bitcast_fusion.7), channel_id=1, source_target_pairs={{0,4},{2,6},{4,0},{6,2},{8,12},{10,14},{12,8},{14,10},{16,20},{18,... | collective-permute-start | bytes 884744 | tf_op jit(solution)/shard_map/ppermute | solution.py:65
  267.0 12.9 %collective-permute-start.36 = (bf16[2,2,24,1664]{3,2,0,1:T(8,128)(2,1)S(1)}, bf16[2,2,24,1664]{3,2,0,1:T(8,128)(2,1)S(1)}, u32[]{:S(2)}, u32[]{:S(2)}) collective-permute-start(bf16[2,2,24,1664]{3,2,0,1:T(8,128)(2,1)S(1)} %dynamic-slice_bitcast_fusion.4), channel_id=1, source_target_pairs={{0,8},{2,10},{4,12},{6,14},{8,0},{10,2},{12,4},{14,6},{16,24},{18,... | collective-permute-start | bytes 958472 | tf_op jit(solution)/shard_map/ppermute | solution.py:65
  277.1 25.4 %collective-permute-start.41 = (bf16[2,2,96,768]{3,2,0,1:T(8,128)(2,1)S(1)}, bf16[2,2,96,768]{3,2,0,1:T(8,128)(2,1)S(1)}, u32[]{:S(2)}, u32[]{:S(2)}) collective-permute-start(bf16[2,2,96,768]{3,2,0,1:T(8,128)(2,1)S(1)} %maximum_select_fusion.11), channel_id=1, source_target_pairs={{0,4},{2,6},{4,0},{6,2},{8,12},{10,14},{12,8},{14,10},{16,20},{18,... | collective-permute-start | bytes 1769480 | tf_op jit(solution)/shard_map/ppermute | solution.py:65
  277.5 26.2 %collective-permute-start.40 = (bf16[2,2,48,1536]{3,2,0,1:T(8,128)(2,1)S(1)}, bf16[2,2,48,1536]{3,2,0,1:T(8,128)(2,1)S(1)}, u32[]{:S(2)}, u32[]{:S(2)}) collective-permute-start(bf16[2,2,48,1536]{3,2,0,1:T(8,128)(2,1)S(1)} %maximum_select_fusion.12), channel_id=1, source_target_pairs={{0,8},{2,10},{4,12},{6,14},{8,0},{10,2},{12,4},{14,6},{16,24},{18,... | collective-permute-start | bytes 1769480 | tf_op jit(solution)/shard_map/ppermute | solution.py:65
  279.3 16.3 %collective-permute-start.35 = (bf16[2,24,1536]{2,1,0:T(8,128)(2,1)S(1)}, bf16[2,24,1536]{2,1,0:T(8,128)(2,1)S(1)}, u32[]{:S(2)}, u32[]{:S(2)}) collective-permute-start(bf16[2,24,1536]{2,1,0:T(8,128)(2,1)S(1)} %dynamic-slice_bitcast_fusion.11), channel_id=1, source_target_pairs={{0,8},{2,10},{4,12},{6,14},{8,0},{10,2},{12,4},{14,6},{16,24},{18,... | collective-permute-start | bytes 442376 | tf_op jit(solution)/shard_map/ppermute | solution.py:65
  280.1 25.4 %collective-permute-start.42 = (bf16[2,24,1664]{2,1,0:T(8,128)(2,1)S(1)}, bf16[2,24,1664]{2,1,0:T(8,128)(2,1)S(1)}, u32[]{:S(2)}, u32[]{:S(2)}) collective-permute-start(bf16[2,24,1664]{2,1,0:T(8,128)(2,1)S(1)} %dynamic-slice_bitcast_fusion.10), channel_id=1, source_target_pairs={{0,4},{2,6},{4,0},{6,2},{8,12},{10,14},{12,8},{14,10},{16,20},{18,... | collective-permute-start | bytes 479240 | tf_op jit(solution)/shard_map/ppermute | solution.py:65
  295.7 9.9 %collective-permute-start.39 = (bf16[24,1536]{1,0:T(8,128)(2,1)S(1)}, bf16[24,1536]{1,0:T(8,128)(2,1)S(1)}, u32[]{:S(2)}, u32[]{:S(2)}) collective-permute-start(bf16[24,1536]{1,0:T(8,128)(2,1)S(1)} %dynamic-slice_bitcast_fusion.13), channel_id=1, source_target_pairs={{0,16},{2,18},{4,20},{6,22},{8,24},{10,26},{12,28},{14,30},{16,0},... | collective-permute-start | bytes 221192 | tf_op jit(solution)/shard_map/ppermute | solution.py:65
  303.8 16.2 %collective-permute-start.45 = (bf16[2,2,2,96,768]{4,3,0,1,2:T(8,128)(2,1)}, bf16[2,2,2,96,768]{4,3,0,1,2:T(8,128)(2,1)S(1)}, u32[]{:S(2)}, u32[]{:S(2)}) collective-permute-start(bf16[2,2,2,96,768]{4,3,0,1,2:T(8,128)(2,1)} %maximum_select_fusion.4), channel_id=1, source_target_pairs={{0,2},{2,0},{4,6},{6,4},{8,10},{10,8},{12,14},{14,12},{16,18},{18,... | collective-permute-start | bytes 3538952 | tf_op jit(solution)/shard_map/ppermute | solution.py:65
  305.0 10.2 %collective-permute-start.44 = (bf16[2,2,2,48,1536]{4,3,0,2,1:T(8,128)(2,1)}, bf16[2,2,2,48,1536]{4,3,0,2,1:T(8,128)(2,1)}, u32[]{:S(2)}, u32[]{:S(2)}) collective-permute-start(bf16[2,2,2,48,1536]{4,3,0,2,1:T(8,128)(2,1)} %maximum_select_fusion.5), channel_id=1, source_target_pairs={{0,2},{2,0},{4,6},{6,4},{8,10},{10,8},{12,14},{14,12},{16,18},{18,... | collective-permute-start | bytes 3538952 | tf_op jit(solution)/shard_map/ppermute | solution.py:65
  (26 other events, 201.7 us)
Sparse Core Ops, SparseCore 0:
  17.6 64.5 all-gather.1
where the time goes:
time: 337 us; the launch traced here: 330 us
  Pallas kernels  122 us (36%)
  waiting for transfers between devices  74.8 us (22%)
  starting transfers between devices  40.9 us (12%)
  local copies, waits for them, and re-layouts  31.2 us (9%)
  other arithmetic  30.8 us (9%)
  between operations  15.6 us (5%)
  matrix products  14.7 us (4%)
    ppermute x42, waiting for transfers between devices, swap_dp(): return lax.ppermute(a, 'dp', [(i, i ^ bit) for i in range(count)])  72.9 us
    pallas_call x1, Pallas kernels, run_middle(): call(middle_kernel, count // tile, [rows(tile, width), rows(tile, width),...  40.8 us
    ppermute x42, starting transfers between devices, swap_dp(): return lax.ppermute(a, 'dp', [(i, i ^ bit) for i in range(count)])  35.3 us
    pallas_call x1, Pallas kernels, run_keys_back(): call(keys_back_kernel, count // tile, [rows(tile, wide), rows(tile, width...  20.8 us
    pallas_call x1, Pallas kernels, run_attention_back(): call(attention_back_kernel, count // tile, [rows(tile, width), rows(tile,...  18.9 us
    pallas_call x1, Pallas kernels, run_queries_back(): call(queries_back_kernel, count // tile, [rows(tile, 2 * width), rows(til...  17.1 us
    pallas_call x1, Pallas kernels, run_keys(): call(keys_kernel, count // tile, [rows(tile, width), full(key_weight.shap...  15.7 us
    dot_general x5, matrix products, tn(): lax.dot_general(a, b, (((0,), (0,)), ((), ())), preferred_element_type=F32)  14.7 us
  transfers between devices with their start and end apart: 47, of which 19 were waited for; matrix products, arithmetic and copies ran while one was open for 18% of the time, Pallas kernels for 25%

commit v1 on v0

--- a/solution.py
+++ b/solution.py
@@ -110,23 +110,22 @@
         return self.a.reshape((-1,) + self.tail[1:])
 
 
-class Scatter:
+class Sum:
     def __init__(self, a, order):
-        count = lax.axis_size("dp")
-        self.left = dp_bits()
-        self.a = a.reshape((2,) * len(self.left) + (a.shape[0] // count,) + a.shape[1:])
+        self.a = a
         self.order = list(order)
+        self.done = []
 
     def start(self, *deps):
         bit = self.order[0]
-        axis = self.left.index(bit)
         a = after(self.a, *deps) if deps else self.a
-        self.own = lax.dynamic_index_in_dim(a, mine(bit), axis, False)
-        self.got = swap_dp(lax.dynamic_index_in_dim(a, 1 - mine(bit), axis, False), bit)
+        count = a.shape[0] // 2
+        self.own = lax.dynamic_slice_in_dim(a, mine(bit) * count, count, 0)
+        self.got = swap_dp(lax.dynamic_slice_in_dim(a, (1 - mine(bit)) * count, count, 0), bit)
         return self
 
     def finish(self, *deps):
-        self.left.remove(self.order.pop(0))
+        self.done.append(self.order.pop(0))
         got = after(self.got, *deps) if deps else self.got
         self.a = (self.own.astype(F32) + got.astype(F32)).astype(self.a.dtype)
         return self
@@ -136,10 +135,9 @@
             self.start().finish()
         return self.a
 
-    def start_swap(self, *deps):
+    def start_swap(self, bit, *deps):
         self.own = after(self.a, *deps) if deps else self.a
-        self.bit = self.left[0]
-        self.got = swap_dp(self.own, self.bit)
+        self.got = swap_dp(self.own, bit)
         return self
 
     def finish_swap(self, *deps):
@@ -147,8 +145,15 @@
         self.a = (self.own.astype(F32) + got.astype(F32)).astype(self.a.dtype)
         return self
 
-    def gather(self, order):
-        return Gather(self.a, order, self.left)
+    def start_back(self):
+        self.got = swap_dp(self.a, self.done[-1])
+        return self
+
+    def finish_back(self, *deps):
+        got = after(self.got, *deps) if deps else self.got
+        a = join_pair(self.a, got, mine(self.done.pop()), 0)
+        self.a = a.reshape((-1,) + a.shape[2:])
+        return self
 
 
 class TableSum:
@@ -212,27 +217,73 @@
     return jnp.exp2(nn(lhs, table) * LOG2E - 4.0)
 
 
-def each_small(flags, t, slot, body):
-    limit = slot.shape[0] - WINDOW
-
-    def one(j, carry):
-        first = flags[t, j]
-        final = flags[t, SLOTS + j]
-        begin = first // 16 * 16
-
-        def window(i, carry):
-            wanted = begin + i * WINDOW
-            start = pl.multiple_of(jnp.minimum(wanted, limit), 16)
-            rows = pl.ds(start, WINDOW)
-            index = lax.broadcasted_iota(jnp.int32, (WINDOW, 128), 0) + start
-            body(rows, jnp.logical_and(slot[rows, :] == j, index >= wanted), j)
+class Documents:
+    def __init__(self, meta, info, tile):
+        self.meta, self.info, self.tile = meta, info, tile
+        self.t = pl.program_id(0)
+
+    def setup(self):
+        meta, info = self.meta, self.info
+        edges = [-meta[SLOTS]]
+        for d in range(SLOTS):
+            edges.append(edges[-1] + meta[d])
+        most, longest = meta[0], jnp.int32(0)
+        for d in range(1, SLOTS):
+            longest = jnp.where(meta[d] > most, d, longest)
+            most = jnp.maximum(most, meta[d])
+        start, stop = edges[0], edges[1]
+        for d in range(1, SLOTS):
+            start = jnp.where(longest == d, edges[d], start)
+            stop = jnp.where(longest == d, edges[d + 1], stop)
+        info[0] = start
+        info[SLOTS] = stop
+        for j in range(1, SLOTS):
+            before = longest > j - 1
+            info[j] = jnp.where(before, edges[j - 1], edges[j])
+            info[SLOTS + j] = jnp.where(before, edges[j], edges[j + 1])
+        info[2 * SLOTS] = edges[SLOTS]
+
+    def slow(self):
+        first = self.t * self.tile
+        inside = jnp.logical_and(self.info[0] <= first, self.info[SLOTS] >= first + self.tile)
+        return jnp.logical_not(inside)
+
+    def present(self, j):
+        rows = self.tile * pl.num_programs(0)
+        return jnp.maximum(self.info[j], 0) < jnp.minimum(self.info[SLOTS + j], rows)
+
+    def places(self, first, rows):
+        return lax.broadcasted_iota(jnp.int32, (rows, 128), 0) + (self.t * self.tile + first)
+
+    def main(self):
+        place = self.places(0, self.tile)
+        return jnp.logical_and(place >= self.info[0], place < self.info[SLOTS])
+
+    def live(self):
+        return self.places(0, self.tile) < self.info[2 * SLOTS]
+
+    def each_small(self, body):
+        limit = self.tile - WINDOW
+        base = self.t * self.tile
+
+        def one(j, carry):
+            first = jnp.clip(self.info[j] - base, 0, self.tile)
+            final = jnp.clip(self.info[SLOTS + j] - base, 0, self.tile)
+            begin = first // 16 * 16
+
+            def window(i, carry):
+                wanted = begin + i * WINDOW
+                start = pl.multiple_of(jnp.minimum(wanted, limit), 16)
+                place = lax.broadcasted_iota(jnp.int32, (WINDOW, 128), 0) + start
+                low = jnp.maximum(first, wanted)
+                body(pl.ds(start, WINDOW), jnp.logical_and(place >= low, place < final), j)
+                return carry
+
+            count = jnp.where(final > first, (final - begin + WINDOW - 1) // WINDOW, 0)
+            lax.fori_loop(0, count, window, 0)
             return carry
 
-        count = jnp.where(final > first, (final - begin + WINDOW - 1) // WINDOW, 0)
-        lax.fori_loop(0, count, window, 0)
-        return carry
-
-    lax.fori_loop(1, SLOTS, one, 0)
+        lax.fori_loop(1, SLOTS, one, 0)
 
 
 def pack_tables(table, base, acc, macc):
@@ -264,7 +315,7 @@
             tabs[p, 128 + k * 64 : 192 + k * 64, span] = mass.astype(BF16)
 
 
-def copy_small(flags, source, target, sems):
+def copy_small(docs, source, target, sems):
     stride = source.shape[0] // (SLOTS - 1)
 
     def part(j):
@@ -273,13 +324,13 @@
 
     for j in range(1, SLOTS):
 
-        @pl.when(flags[0, 2 * SLOTS + j] > 0)
+        @pl.when(docs.present(j))
         def _():
             part(j).start()
 
     for j in range(1, SLOTS):
 
-        @pl.when(flags[0, 2 * SLOTS + j] > 0)
+        @pl.when(docs.present(j))
         def _():
             part(j).wait()
 
@@ -310,29 +361,31 @@
 
 
 def keys_kernel(
-    flags, x, key_weight, value_weight, bias, table, slot,
+    meta, x, key_weight, value_weight, bias, table,
     phi, values, scaled_out, main, small_out,
-    acc, macc, sacc, smacc, small, sems,
+    acc, macc, sacc, smacc, small, sems, info,
 ):
     t = pl.program_id(0)
+    docs = Documents(meta, info, x.shape[0])
     pairs = table.shape[0]
     width = pairs * 128
-    slow = flags[t, 0] == 0
 
     @pl.when(t == 0)
     def _():
+        docs.setup()
         acc[...] = jnp.zeros_like(acc)
         macc[...] = jnp.zeros_like(macc)
 
         for j in range(1, SLOTS):
 
-            @pl.when(flags[0, 2 * SLOTS + j] > 0)
+            @pl.when(docs.present(j))
             def _():
                 sacc[j - 1] = jnp.zeros_like(sacc[j - 1])
                 smacc[j - 1] = jnp.zeros_like(smacc[j - 1])
 
-    keys = nn(x[...], key_weight[:, :width]) + bias[:, :width]
-    values[...] = (nn(x[...], value_weight[...]) + bias[:, width:]).astype(BF16)
+    slow = docs.slow()
+    keys = nn(x[...], key_weight[:, :width]) + bias[:, width : 2 * width]
+    values[...] = (nn(x[...], value_weight[...]) + bias[:, 2 * width :]).astype(BF16)
     for p in range(pairs):
         scaled = keys[:, p * 128 : (p + 1) * 128] * 64 ** (-0.25)
         scaled_out[:, p * 128 : (p + 1) * 128] = scaled.astype(BF16)
@@ -347,7 +400,7 @@
 
     @pl.when(slow)
     def _():
-        mask = slot[...] == 0
+        mask = docs.main()
         for p in range(pairs):
             part = phi[:, p * 512 : (p + 1) * 512]
             acc[p] += tn(masked(mask, values[:, p * 128 : (p + 1) * 128]).astype(BF16), part)
@@ -360,7 +413,7 @@
                 sacc[j - 1, p] += tn(value, part)
                 smacc[j - 1, p] += fold_rows(masked(mask, part))
 
-        each_small(flags, t, slot, body)
+        docs.each_small(body)
 
     @pl.when(t == pl.num_programs(0) - 1)
     def _():
@@ -368,16 +421,16 @@
 
         for j in range(1, SLOTS):
 
-            @pl.when(flags[0, 2 * SLOTS + j] > 0)
+            @pl.when(docs.present(j))
             def _():
                 pack_tables(small, (j - 1) * main.shape[0], sacc.at[j - 1], smacc.at[j - 1])
 
-        copy_small(flags, small, small_out, sems)
-
-
-def queries_kernel(flags, x, weight, bias, table, select, phi, scaled_out, chosen):
+        copy_small(docs, small, small_out, sems)
+
+
+def queries_kernel(meta, x, weight, bias, table, select, phi, scaled_out, chosen):
     pairs = table.shape[0]
-    query = nn(x[...], weight[...]) + bias[...]
+    query = nn(x[...], weight[...]) + bias[:, : pairs * 128]
     chosen[...] = nn(x[...], select[...]).astype(BF16)
     for p in range(pairs):
         scaled = query[:, p * 128 : (p + 1) * 128] * 64 ** (-0.25)
@@ -399,16 +452,17 @@
 
 
 def middle_kernel(
-    flags, x, cot, slot, phi, main, small_in,
+    meta, x, cot, phi, main, small_in,
     out_weight, up_own, up_here, up_there, down_own, down_here, down_there, bias_own, bias_other, vectors,
     layer_out, hidden_grad, normed_out, inverse_out, att_out, invden_out,
     active_out, dup_out, hidden_out, dffn_out, sums, up_sum,
-    tabs, spread, gates, other, up_other, down_other, small, sems, half_sems,
+    tabs, spread, gates, other, up_other, down_other, small, sems, half_sems, info,
 ):
     t = pl.program_id(0)
+    docs = Documents(meta, info, x.shape[0])
     pairs = tabs.shape[0]
     width = pairs * 128
-    core = flags[0, 3 * SLOTS]
+    core = meta[SLOTS + 1]
 
     def halves():
         copies = []
@@ -426,15 +480,16 @@
     def _():
         for copy in halves():
             copy.start()
+        docs.setup()
         fill_tables(tabs, main, True)
-        copy_small(flags, small_in, small, sems)
+        copy_small(docs, small_in, small, sems)
         sums[...] = jnp.zeros_like(sums)
         up_sum[...] = jnp.zeros_like(up_sum)
 
     for p in range(pairs):
         spread[:, p * 256 : (p + 1) * 256] = nt(phi[:, p * 512 : (p + 1) * 512], tabs[p])
 
-    @pl.when(flags[t, 0] == 0)
+    @pl.when(docs.slow())
     def _():
         def body(rows, mask, j):
             wide = jnp.concatenate([mask] * 2, axis=1)
@@ -443,9 +498,9 @@
                 old = spread[rows, p * 256 : (p + 1) * 256]
                 spread[rows, p * 256 : (p + 1) * 256] = jnp.where(wide, got, old)
 
-        each_small(flags, t, slot, body)
-
-    live = slot[...] < SLOTS
+        docs.each_small(body)
+
+    live = docs.live()
     for p in range(pairs):
         numerator = spread[:, p * 256 : p * 256 + 128]
         denominator = spread[:, p * 256 + 128 : (p + 1) * 256]
@@ -506,22 +561,23 @@
 
 
 def attention_back_kernel(
-    flags, hidden_grad, normed, inverse, att, invden, phi, slot, out_weight, gain, select, more, up_sum,
+    meta, hidden_grad, normed, inverse, att, invden, phi, out_weight, gain, select, more, up_sum,
     dfirst_out, dbranch_out, mixed, chosen, sums, main, small_out,
-    acc, sacc, small, sems,
+    acc, sacc, small, sems, info,
 ):
     t = pl.program_id(0)
+    docs = Documents(meta, info, att.shape[0])
     pairs = acc.shape[0]
-    slow = flags[t, 0] == 0
 
     @pl.when(t == 0)
     def _():
+        docs.setup()
         acc[...] = jnp.zeros_like(acc)
         sums[...] = jnp.zeros_like(sums)
 
         for j in range(1, SLOTS):
 
-            @pl.when(flags[0, 2 * SLOTS + j] > 0)
+            @pl.when(docs.present(j))
             def _():
                 sacc[j - 1] = jnp.zeros_like(sacc[j - 1])
 
@@ -535,6 +591,7 @@
     dbranch_out[...] = dbranch
     sums[16:24, :] += fold_rows(dbranch.astype(F32))
     chosen[...] = nn(att[...], select[...]).astype(BF16)
+    slow = docs.slow()
     datt = nt(dbranch, out_weight[...])
     ratio = datt * invden[...]
     dden = -ratio * att[...].astype(F32)
@@ -549,7 +606,7 @@
 
     @pl.when(slow)
     def _():
-        mask = slot[...] == 0
+        mask = docs.main()
         for p in range(pairs):
             part = masked(mask, mixed[:, p * 256 : (p + 1) * 256]).astype(BF16)
             acc[p] += tn(part, phi[:, p * 512 : (p + 1) * 512])
@@ -559,7 +616,7 @@
                 part = masked(mask, mixed[rows, p * 256 : (p + 1) * 256]).astype(BF16)
                 sacc[j - 1, p] += tn(part, phi[rows, p * 512 : (p + 1) * 512])
 
-        each_small(flags, t, slot, body)
+        docs.each_small(body)
 
     @pl.when(t == pl.num_programs(0) - 1)
     def _():
@@ -574,11 +631,11 @@
 
         for j in range(1, SLOTS):
 
-            @pl.when(flags[0, 2 * SLOTS + j] > 0)
+            @pl.when(docs.present(j))
             def _():
                 pack_tables(small, (j - 1) * (pairs * 128 + 16), sacc.at[j - 1], None)
 
-        copy_small(flags, small, small_out, sems)
+        copy_small(docs, small, small_out, sems)
 
 
 def feature_back(rows, p, grad, phi, scaled, table):
@@ -594,16 +651,18 @@
 
 
 def queries_back_kernel(
-    flags, mixed, phi, scaled, slot, main, small_in, table, weight, dfirst,
-    dquery_out, partial_out, sums, tabs, small, sems,
+    meta, mixed, phi, scaled, main, small_in, table, weight, dfirst,
+    dquery_out, partial_out, sums, tabs, small, sems, info,
 ):
     t = pl.program_id(0)
+    docs = Documents(meta, info, phi.shape[0])
     pairs = tabs.shape[0]
 
     @pl.when(t == 0)
     def _():
+        docs.setup()
         fill_tables(tabs, main, True)
-        copy_small(flags, small_in, small, sems)
+        copy_small(docs, small_in, small, sems)
         sums[...] = jnp.zeros_like(sums)
 
     for p in range(pairs):
@@ -611,7 +670,7 @@
         du = feature_back(slice(None), p, grad, phi, scaled, table)
         dquery_out[:, p * 128 : (p + 1) * 128] = du.astype(BF16)
 
-    @pl.when(flags[t, 0] == 0)
+    @pl.when(docs.slow())
     def _():
         def body(rows, mask, j):
             for p in range(pairs):
@@ -620,24 +679,26 @@
                 du = feature_back(rows, p, grad, phi, scaled, table)
                 store_some(dquery_out, rows, slice(p * 128, (p + 1) * 128), mask, du)
 
-        each_small(flags, t, slot, body)
+        docs.each_small(body)
 
     sums[...] += fold_rows(dquery_out[...].astype(F32))
     partial_out[...] = dfirst[...] + nt(dquery_out[...], weight[...])
 
 
 def keys_back_kernel(
-    flags, phi, values, scaled, slot, main, small_in, table, key_weight, value_weight, partial_in,
-    djoint_out, tokens_out, sums, tabs, small, sems,
+    meta, phi, values, scaled, main, small_in, table, key_weight, value_weight, partial_in,
+    djoint_out, tokens_out, sums, tabs, small, sems, info,
 ):
     t = pl.program_id(0)
+    docs = Documents(meta, info, phi.shape[0])
     pairs = tabs.shape[0]
     width = pairs * 128
 
     @pl.when(t == 0)
     def _():
+        docs.setup()
         fill_tables(tabs, main, False)
-        copy_small(flags, small_in, small, sems)
+        copy_small(docs, small_in, small, sems)
         sums[...] = jnp.zeros_like(sums)
 
     def extended(rows, p):
@@ -651,9 +712,9 @@
         dvalue = nt(phi[:, p * 512 : (p + 1) * 512], tabs[p, :128, :])
         djoint_out[:, width + p * 128 : width + (p + 1) * 128] = dvalue.astype(BF16)
 
-    @pl.when(flags[t, 0] == 0)
-    def _():
-        live = slot[...] < SLOTS
+    @pl.when(docs.slow())
+    def _():
+        live = docs.live()
         for p in range(2 * pairs):
             part = djoint_out[:, p * 128 : (p + 1) * 128]
             djoint_out[:, p * 128 : (p + 1) * 128] = masked(live, part).astype(BF16)
@@ -668,7 +729,7 @@
                 span = slice(width + p * 128, width + (p + 1) * 128)
                 store_some(djoint_out, rows, span, mask, dvalue)
 
-        each_small(flags, t, slot, body)
+        docs.each_small(body)
 
     sums[...] += fold_rows(djoint_out[...].astype(F32))
     tokens_out[...] = (
@@ -698,7 +759,7 @@
     return pltpu.VMEM(((SLOTS - 1) * (width + 16), 256), BF16)
 
 
-def run_keys(tile, flags, tokens, key_weight, value_weight, bias, table, slots):
+def run_keys(tile, meta, tokens, key_weight, value_weight, bias, table):
     count, width = tokens.shape
     pairs = table.shape[0]
     wide = pairs * 512
@@ -706,8 +767,8 @@
         keys_kernel,
         count // tile,
         [
-            rows(tile, width), full(key_weight.shape), full((width, width)), full((1, 2 * width)),
-            full(table.shape), rows(tile, 128),
+            rows(tile, width), full(key_weight.shape), full((width, width)), full(bias.shape),
+            full(table.shape),
         ],
         [
             (rows(tile, wide), (count, wide), BF16),
@@ -722,12 +783,13 @@
             pltpu.VMEM((SLOTS - 1, pairs, 8, 512), F32),
             small_scratch(width),
             pltpu.SemaphoreType.DMA((SLOTS - 1,)),
+            pltpu.SMEM((3 * SLOTS,), jnp.int32),
         ],
         10e9,
-    )(flags, tokens, key_weight, value_weight, bias, table, slots)
-
-
-def run_queries(tile, flags, tokens, weight, bias, table, select):
+    )(meta, tokens, key_weight, value_weight, bias, table)
+
+
+def run_queries(tile, meta, tokens, weight, bias, table, select):
     count, width = tokens.shape
     wide = table.shape[0] * 512
     own_rows = select.shape[1]
@@ -735,7 +797,7 @@
         queries_kernel,
         count // tile,
         [
-            rows(tile, width), column((width, width), 0), full((1, width)), full(table.shape),
+            rows(tile, width), column((width, width), 0), full(bias.shape), full(table.shape),
             full((width, own_rows)),
         ],
         [
@@ -745,11 +807,11 @@
         ],
         [],
         6e9,
-    )(flags, tokens, weight, bias, table, select)
+    )(meta, tokens, weight, bias, table, select)
 
 
 def run_middle(
-    tile, flags, tokens, cotangent, slots, phi, moments, small, query_out, up_own, up_here, up_there,
+    tile, meta, tokens, cotangent, phi, moments, small, query_out, up_own, up_here, up_there,
     down_own, down_here, down_there, bias_own, bias_other, vectors,
 ):
     count, width = tokens.shape
@@ -759,7 +821,7 @@
     return call(
         middle_kernel,
         count // tile,
-        [rows(tile, width), rows(tile, width), rows(tile, 128), rows(tile, wide)]
+        [rows(tile, width), rows(tile, width), rows(tile, wide)]
         + table_ins(width)
         + [
             column((width, width), 1),
@@ -797,16 +859,17 @@
             small_scratch(width),
             pltpu.SemaphoreType.DMA((SLOTS - 1,)),
             pltpu.SemaphoreType.DMA((4,)),
+            pltpu.SMEM((3 * SLOTS,), jnp.int32),
         ],
         30e9,
     )(
-        flags, tokens, cotangent, slots, phi, moments, small, query_out, up_own, up_here, up_there,
+        meta, tokens, cotangent, phi, moments, small, query_out, up_own, up_here, up_there,
         down_own, down_here, down_there, bias_own, bias_other, vectors,
     )
 
 
 def run_attention_back(
-    tile, flags, hidden_grad, normed, inverse, att, invden, phi, slots, query_out, gain, select, sums, up_sum
+    tile, meta, hidden_grad, normed, inverse, att, invden, phi, query_out, gain, select, sums, up_sum
 ):
     count, width = att.shape
     wide = phi.shape[1]
@@ -818,7 +881,7 @@
         count // tile,
         [
             rows(tile, width), rows(tile, width), rows(tile, 128), rows(tile, width), rows(tile, width),
-            rows(tile, wide), rows(tile, 128), column((width, width), 1), full((1, width)), full((width, own_rows)),
+            rows(tile, wide), column((width, width), 1), full((1, width)), full((width, own_rows)),
             full((24, width)), full((8, half)),
         ],
         [
@@ -834,20 +897,21 @@
             pltpu.VMEM((SLOTS - 1, pairs, 256, 512), F32),
             small_scratch(width),
             pltpu.SemaphoreType.DMA((SLOTS - 1,)),
+            pltpu.SMEM((3 * SLOTS,), jnp.int32),
         ],
         6e9,
     )(
-        flags, hidden_grad, normed, inverse, att, invden, phi, slots, query_out, gain, select, sums, up_sum
-    )
-
-
-def run_queries_back(tile, flags, mixed, phi, scaled, slots, moments, small, table, weight, dfirst):
+        meta, hidden_grad, normed, inverse, att, invden, phi, query_out, gain, select, sums, up_sum
+    )
+
+
+def run_queries_back(tile, meta, mixed, phi, scaled, moments, small, table, weight, dfirst):
     count, width = scaled.shape
     wide = phi.shape[1]
     return call(
         queries_back_kernel,
         count // tile,
-        [rows(tile, 2 * width), rows(tile, wide), rows(tile, width), rows(tile, 128)]
+        [rows(tile, 2 * width), rows(tile, wide), rows(tile, width)]
         + table_ins(width)
         + [full(table.shape), column((width, width), 0), rows(tile, width)],
         [
@@ -855,20 +919,25 @@
             (rows(tile, width), (count, width), F32),
             (held((8, width)), (8, width), F32),
         ],
-        [table_scratch(width), small_scratch(width), pltpu.SemaphoreType.DMA((SLOTS - 1,))],
+        [
+            table_scratch(width),
+            small_scratch(width),
+            pltpu.SemaphoreType.DMA((SLOTS - 1,)),
+            pltpu.SMEM((3 * SLOTS,), jnp.int32),
+        ],
         8e9,
-    )(flags, mixed, phi, scaled, slots, moments, small, table, weight, dfirst)
+    )(meta, mixed, phi, scaled, moments, small, table, weight, dfirst)
 
 
 def run_keys_back(
-    tile, flags, phi, values, scaled, slots, moments, small, table, key_weight, value_weight, partial
+    tile, meta, phi, values, scaled, moments, small, table, key_weight, value_weight, partial
 ):
     count, width = scaled.shape
     wide = phi.shape[1]
     return call(
         keys_back_kernel,
         count // tile,
-        [rows(tile, wide), rows(tile, width), rows(tile, width), rows(tile, 128)]
+        [rows(tile, wide), rows(tile, width), rows(tile, width)]
         + table_ins(width)
         + [full(table.shape), full(key_weight.shape), full((width, width)), rows(tile, width)],
         [
@@ -880,10 +949,11 @@
             table_scratch(width),
             small_scratch(width),
             pltpu.SemaphoreType.DMA((SLOTS - 1,)),
+            pltpu.SMEM((3 * SLOTS,), jnp.int32),
         ],
         12e9,
     )(
-        flags, phi, values, scaled, slots, moments, small, table, key_weight, value_weight, partial,
+        meta, phi, values, scaled, moments, small, table, key_weight, value_weight, partial,
     )
 
 
@@ -896,81 +966,77 @@
     heads, head_size, feature_count = feature_maps.shape
     pairs = heads // 2
     half = up_weight.shape[1]
-    tile = TILE
-    tiles = count // tile
     rank = lax.axis_index("dp")
     dp = lax.axis_size("dp")
     mp = lax.axis_size("mp")
     mp_rank = lax.axis_index("mp")
 
-    lengths = document_lengths[0]
-    ends = jnp.cumsum(lengths)
-    place = rank * count + jnp.arange(count, dtype=jnp.int32)
-    document = jnp.sum((ends[None, :] <= place[:, None]).astype(jnp.int32), axis=1)
-    longest = jnp.argmax(lengths).astype(jnp.int32)
-    slot = jnp.where(
-        document == longest,
-        0,
-        jnp.where(document >= SLOTS, SLOTS, jnp.where(document < longest, document + 1, document)),
-    )
-    slots = jnp.broadcast_to(slot[:, None], (count, 128))
-    order = jnp.arange(SLOTS, dtype=jnp.int32)
-    which = jnp.where(order - 1 < longest, order - 1, order)
-    starts = jnp.where(which > 0, ends[jnp.maximum(which - 1, 0)], 0)
-    stops = ends[jnp.maximum(which, 0)]
-    base = rank * count + jnp.arange(tiles, dtype=jnp.int32)[:, None] * tile
-    all_main = jnp.max(slot.reshape(tiles, tile), axis=1, keepdims=True) == 0
-    starts_in = jnp.clip(starts[None, :] - base, 0, tile)
-    stops_in = jnp.clip(stops[None, :] - base, 0, tile)
-    present = jnp.max((stops_in > starts_in).astype(jnp.int32), axis=0, keepdims=True)
-    flags = jnp.concatenate(
-        [
-            all_main.astype(jnp.int32),
-            starts_in[:, 1:],
-            stops_in,
-            jnp.broadcast_to(present, (tiles, SLOTS)),
-            jnp.broadcast_to(mine(1).astype(jnp.int32), (tiles, SLOTS)),
-        ],
-        axis=1,
-    )
-
     shard = joint_weight.shape[0]
+    small_vectors = [joint_bias, output_bias, first_gain, first_shift, second_gain, second_shift]
+    stacks = -(-len(small_vectors) // shard)
+    small_vectors = jnp.stack([jnp.pad(v, (0, 128 - v.shape[0])) for v in small_vectors])
+    small_vectors = jnp.pad(small_vectors, ((0, stacks * shard - small_vectors.shape[0]), (0, 0)))
     small_vectors = jnp.concatenate(
-        [joint_bias, output_bias, first_gain, first_shift, second_gain, second_shift]
-    )
-    vector_size = small_vectors.shape[0]
-    lines = -(-vector_size // 128)
-    small_vectors = jnp.pad(small_vectors, (0, lines * 128 - vector_size)).reshape(lines, 128)
-    small_vectors = jnp.pad(small_vectors, ((0, shard - lines), (0, 0)))
-    shards = jnp.concatenate([joint_weight[:, width:], small_vectors], axis=1)
-    query_out = lax.all_gather(
-        jnp.concatenate([joint_weight[:, :width], output_weight], axis=1), ("dp", "mp"), axis=0, tiled=True
-    )
-    shards = join_pair(shards, swap_mp(shards), mp_rank, 0).reshape(2 * shard, -1)
-    key_chain = Gather(
-        jnp.concatenate([shards[:, :width], shards[:, 2 * width :]], axis=1), far_first()
-    )
-    value_chain = Gather(shards[:, width : 2 * width], near_first())
-
+        [small_vectors[i * shard : (i + 1) * shard] for i in range(stacks)], axis=1
+    )
     core = mine(1)
 
     def own_part(a):
         return lax.dynamic_slice_in_dim(a, core * (a.shape[0] // 2), a.shape[0] // 2, 0)
 
+    far_weight = swap_mp(joint_weight)
+    far_vectors = swap_mp(small_vectors)
+
+    def over_x(own, other):
+        return join_pair(own, other, mp_rank, 0).reshape(2 * shard, -1)
+
+    value_chain = Gather(
+        over_x(joint_weight[:, 2 * width :], far_weight[:, 2 * width :]), near_first()
+    ).start()
+    key_chain = Gather(
+        jnp.concatenate(
+            [
+                over_x(joint_weight[:, width : 2 * width], far_weight[:, width : 2 * width]),
+                over_x(small_vectors, far_vectors),
+            ],
+            axis=1,
+        ),
+        far_first(),
+    ).start()
+    early = key_chain.a
+    query_out = lax.all_gather(
+        after(jnp.concatenate([joint_weight[:, :width], output_weight], axis=1), early),
+        ("dp", "mp"),
+        axis=0,
+        tiled=True,
+    )
+    up_here = swap_mp(after(own_part(up_weight), early))
+    down_here = swap_mp(after(own_part(down_weight), early))
+    meta = jnp.concatenate(
+        [
+            document_lengths[0],
+            jnp.stack([rank * count, core]).astype(jnp.int32),
+            jnp.zeros((SLOTS - 2,), jnp.int32),
+        ]
+    )
+
+    key_chain.finish()
+    value_chain.finish()
     while key_chain.order:
+        value_chain.start()
         key_chain.start()
-        value_chain.start()
-        if len(key_chain.order) == len(dp_bits()):
-            up_here = swap_mp(after(own_part(up_weight), shards))
-            down_here = swap_mp(after(own_part(down_weight), up_here))
         key_chain.finish()
         value_chain.finish()
     key_weight = key_chain.result()
     value_weight = value_chain.result()
 
-    vectors_all = key_weight[:, width:].reshape(dp * mp, shard, 128)[:, :lines].reshape(dp * mp, -1)
-    bias_part = joint_bias.shape[0]
-    joint_offset = vectors_all[:, :bias_part].reshape(1, -1).astype(F32)
+    vectors_all = key_weight[:, width:].reshape(dp * mp, shard, stacks * 128)
+
+    def vector(i, size):
+        start = i // shard * 128
+        return vectors_all[:, i % shard, start : start + size].reshape(-1).astype(F32)
+
+    joint_offset = vector(0, joint_bias.shape[0])[None, :]
     bias_own = up_bias[None, :].astype(F32)
 
     pair_maps = feature_maps.reshape(pairs, 2, head_size, feature_count)
@@ -984,130 +1050,126 @@
         ],
         axis=1,
     )
+    bits = dp_bits()
+    far, middle_bits, near = bits[0], bits[1:-2], bits[-2:-1]
+    owner_order = [1] + near + middle_bits + [far]
     own_rows = width // mp
     index = jnp.arange(own_rows, dtype=jnp.int32)
-    source = index // shard * (shard * mp) + mp_rank * shard + index % shard
+    owner = sum(
+        (index // shard // (dp // 2 >> place)) % 2 * bit for place, bit in enumerate(owner_order)
+    )
+    source = owner * (shard * mp) + mp_rank * shard + index % shard
     select = (jnp.arange(width, dtype=jnp.int32)[:, None] == source[None, :]).astype(BF16)
 
     phi_k, values, scaled_k, moments, small_moments = run_keys(
-        TILE, flags, tokens, key_weight, value_weight, joint_offset[:, width:], table, slots
+        TILE, meta, tokens, key_weight, value_weight, joint_offset, table
     )
 
     up_there = swap_dp(after(up_here, moments), 1)
     down_there = swap_dp(after(down_here, up_there), 1)
     bias_other = swap_mp(after(up_bias, moments)[None, :]).astype(F32)
     vectors_all = after(vectors_all, moments)
-    parts = [
-        vectors_all[:, bias_part + i * shard : bias_part + (i + 1) * shard].reshape(-1).astype(F32)
-        for i in range(5)
-    ]
+    parts = [vector(i, shard) for i in range(1, 6)]
     vectors = jnp.stack(
         [parts[0], parts[1], parts[2], down_bias.astype(F32), parts[3], parts[4], parts[4], parts[4]]
     )
-    bits = dp_bits()
-    far, others = bits[0], bits[1:-1]
+    others = middle_bits + near
     moments_sum = TableSum(moments).add()
     for bit in reversed(others):
         moments_sum.swap(bit).add()
     moments_sum.swap(far)
     phi_q, scaled_q, tokens_own = run_queries(
-        TILE, flags, after(tokens, moments_sum.own), query_out, joint_offset[:, :width], table, select
+        TILE, meta, after(tokens, moments_sum.own), query_out, joint_offset, table, select
     )
     moments = moments_sum.add(phi_q).swap(1).join()
     (
         layer_output, hidden_grad, normed, inverse, att, invden, active, dup, hidden_low, dffn, sums, up_sum,
     ) = run_middle(
-        TILE, flags, tokens, cotangent, slots, phi_q, moments, small_moments, query_out, up_weight,
+        TILE, meta, tokens, cotangent, phi_q, moments, small_moments, query_out, up_weight,
         up_here, up_there, down_weight, down_here, down_there, bias_own, bias_other, vectors,
     )
 
-    near = others[-1:]
-    middle_bits = others[:-1]
-    down_order = [1] + near + middle_bits
-    up_order = [1] + middle_bits + near
-    down_grad = tn(active, dffn).astype(BF16)
-    down = Scatter(down_grad, down_order).start()
-    up_grad = tn(after(hidden_low, down_grad), dup).astype(BF16)
-    down.finish(up_grad)
-    up = Scatter(up_grad, up_order).start(down.a)
-    down.start()
-    up.finish(down.a).start()
-
     dfirst, dbranch, mixed, att_own, first_sums, dmoments, small_dmoments = run_attention_back(
-        TILE, flags, after(hidden_grad, up.a, down.a), normed, inverse, att, invden, phi_q, slots,
-        query_out, vectors[1:2], select, sums, up_sum,
+        TILE, meta, hidden_grad, normed, inverse, att, invden, phi_q, query_out, vectors[1:2],
+        select, sums, up_sum,
     )
 
     dmoments_sum = TableSum(dmoments)
-    down.finish(dmoments)
-    up.finish(down.a)
-    dmoments_sum.add(up.a)
-    for place, bit in enumerate(middle_bits):
+    down_grad = tn(after(active, dmoments), dffn).astype(BF16)
+    down = Sum(down_grad, [1] + near + middle_bits)
+    dmoments_sum.add(down_grad)
+    first_bit = True
+    for bit in middle_bits:
         dmoments_sum.swap(bit)
-        if place == 0:
+        if first_bit:
             down.start(dmoments_sum.own)
-            up.start(dmoments_sum.own)
-            out_grad = tn(after(att_own, dmoments_sum.own), dbranch).astype(BF16)
-            dmoments_sum.add(out_grad)
+            up_grad = tn(after(hidden_low, dmoments_sum.own), dup).astype(BF16)
+            up = Sum(up_grad, [1] + middle_bits + near)
+            down.finish(up_grad)
+            up.start(down.a)
+            down.start()
+            out_grad = tn(after(att_own, up_grad), dbranch).astype(BF16)
+            up.finish(out_grad)
+            dmoments_sum.add(up.a)
+            first_bit = False
         else:
             dmoments_sum.add()
     dmoments_sum.swap(far)
+    up.start(dmoments_sum.own)
     dquery, partial_tokens, query_sums = run_queries_back(
-        TILE, flags, mixed, phi_q, scaled_q, slots, moments, small_moments, table, query_out,
-        after(dfirst, dmoments_sum.own),
+        TILE, meta, mixed, phi_q, scaled_q, moments, small_moments, table, query_out,
+        after(dfirst, dmoments_sum.own, up.own),
     )
     dmoments_sum.add(dquery).swap(near[0])
-    down.finish(dmoments_sum.own)
+    down.finish(dmoments_sum.own).start()
+    up.finish(down.a).start()
+    query_grad = tn(after(tokens_own, up.a), dquery).astype(BF16)
+    dmoments_sum.add(query_grad).swap(1)
+    query_out_sum = Sum(jnp.concatenate([query_grad, out_grad], axis=1), owner_order)
+    query_out_sum.start(dmoments_sum.own)
+    dmoments = dmoments_sum.join(query_out_sum.own)
+    down.finish(query_out_sum.own)
     up.finish(down.a)
     while down.order:
         down.start().finish()
         up.start().finish()
-    down.start_swap()
-    up.start_swap(down.a)
-    query_grad = tn(after(tokens_own, dmoments_sum.own), dquery).astype(BF16)
-    query_out_grad = Scatter(jnp.concatenate([query_grad, out_grad], axis=1), down_order + [far])
-    query_out_grad.start(dmoments_sum.add(query_grad).own)
-    dmoments_sum.swap(1)
-    query_out_grad.finish(dmoments_sum.own).start()
-    dmoments = dmoments_sum.join(query_out_grad.a)
+    down.start_swap(far)
+    up.start_swap(far, down.a)
+    query_out_sum.finish(up.a).start()
     dkey_value, tokens_grad, key_sums = run_keys_back(
-        TILE, flags, phi_k, values, scaled_k, slots, dmoments, small_dmoments, table, key_weight,
-        value_weight, after(partial_tokens, query_out_grad.a),
-    )
-    key_value_grad = tn(tokens_own, dkey_value).astype(BF16)
+        TILE, meta, phi_k, values, scaled_k, dmoments, small_dmoments, table, key_weight,
+        value_weight, after(partial_tokens, query_out_sum.own, up.own, down.own),
+    )
+    down.finish_swap(dkey_value).start_back()
+    up.finish_swap(down.a).start_back()
+    key_value_grad = tn(after(tokens_own, up.a), dkey_value).astype(BF16)
     biases = jnp.concatenate([jnp.sum(query_sums, axis=0), jnp.sum(key_sums, axis=0)])
+    per_owner = biases.shape[0] // dp
+    biases = biases.reshape((2,) * len(bits) + (-1,))
+    biases = biases.transpose([bits.index(bit) for bit in owner_order] + [len(bits)])
     biases = biases.reshape(dp * shard, -1)
     bias_columns = biases.shape[1]
     biases = jnp.pad(biases, ((0, 0), (0, 128 - bias_columns))).astype(BF16)
-    key_value_sum = Scatter(jnp.concatenate([key_value_grad, biases], axis=1), up_order + [far]).start()
-
-    down.finish_swap(dkey_value)
-    up.finish_swap(down.a)
-    down = down.gather(middle_bits[::-1] + near + [1]).start()
-    up = up.gather(near + middle_bits[::-1] + [1]).start()
-    key_value_sum.finish(up.a, down.a).start()
-    query_out_grad.finish(key_value_sum.a).start()
-    down.finish(query_out_grad.a).start()
-    up.finish(down.a).start()
-    key_value_sum.finish(up.a)
-    query_out_grad.finish(key_value_sum.a)
-    while down.order:
+    key_value_sum = Sum(jnp.concatenate([key_value_grad, biases], axis=1), owner_order).start()
+    query_out_sum.finish(key_value_sum.own).start()
+    key_value_sum.finish(query_out_sum.own).start()
+    while len(down.done) > 1:
+        down.finish_back(key_value_sum.own).start_back()
+        up.finish_back(down.a).start_back()
+        if query_out_sum.order:
+            query_out_sum.finish(up.a)
+            if query_out_sum.order:
+                query_out_sum.start()
+        key_value_sum.finish(up.a)
         if key_value_sum.order:
             key_value_sum.start()
-        if query_out_grad.order:
-            query_out_grad.start()
-        down.finish(key_value_sum.a)
-        up.finish(down.a)
-        if down.order:
-            down.start()
-            up.start()
-        if query_out_grad.got is not None and query_out_grad.order:
-            query_out_grad.finish(up.a)
-        if key_value_sum.order:
-            key_value_sum.finish(up.a)
-    down_total = down.result()
-    up_total = up.result()
-    query_out_total = query_out_grad.rest().astype(F32)
+    down_total = down.finish_back(key_value_sum.own).a
+    up_total = up.finish_back(down_total).a
+    if query_out_sum.order:
+        query_out_sum.finish(up.a)
+    query_out_total = query_out_sum.rest().astype(F32)
+    if key_value_sum.order:
+        key_value_sum.finish(up.a)
     key_value_total = key_value_sum.rest().astype(F32)
 
     extra = dmoments[width + 16 :].reshape(-1).astype(F32)

time: 337 us -> 320 us (0.950)
  starting transfers between devices: 40.9 us -> 67.1 us
  Pallas kernels: 122 us -> 104 us
  waiting for transfers between devices: 74.8 us -> 61.1 us
  local copies, waits for them, and re-layouts: 31.2 us -> 21.7 us
    ppermute x42, starting transfers between devices: 35.3 us -> 60.4 us  [swap_dp(): return lax.ppermute(a, 'dp', [(i, i ^ bit) for i in range(count)])]
    ppermute x42, waiting for transfers between devices: 72.9 us -> 57.7 us  [swap_dp(): return lax.ppermute(a, 'dp', [(i, i ^ bit) for i in range(count)])]
    pallas_call x1, Pallas kernels: 20.8 us -> 15.8 us  [run_keys_back(): call(keys_back_kernel, count // tile, [rows(tile, wide), rows(tile, width...]
    concatenate x2 -> x0, local copies, waits for them, and re-layouts: 4.79 us -> none  [the longest x1 4.14 us: local(): jnp.concatenate([joint_bias, output_bias, first_gain, first_shift, second...]
    convert_element_type x9 -> x6, local copies, waits for them, and re-layouts: 5.86 us -> 1.3 us  [vector(): return vectors_all[:, i % shard, start:start + size].reshape(-1).astype(F32)]
    pallas_call x1, Pallas kernels: 17.1 us -> 12.9 us  [run_queries_back(): call(queries_back_kernel, count // tile, [rows(tile, 2 * width), rows(til...]
    pallas_call x1, Pallas kernels: 18.9 us -> 15.2 us  [run_attention_back(): call(attention_back_kernel, count // tile, [rows(tile, width), rows(tile,...]
    squeeze x13 -> x0, local copies, waits for them, and re-layouts: 3.68 us -> none  [start(): lax.dynamic_index_in_dim(a, 1 - mine(bit), axis, False)]
  transfers between devices with their start and end apart: 47 -> 48, of which waited for: 19 -> 23; matrix products, arithmetic and copies ran while one was open for 18% -> 17% of each run, Pallas kernels for 25% -> 16%
where the time goes in v1:
time: 320 us; the launch traced here: 313 us
  Pallas kernels  104 us (32%)
  starting transfers between devices  67.1 us (21%)
  waiting for transfers between devices  61.1 us (19%)
  other arithmetic  28.9 us (9%)
  local copies, waits for them, and re-layouts  21.7 us (7%)
  matrix products  15.5 us (5%)
  between operations  15.4 us (5%)
    ppermute x42, starting transfers between devices, swap_dp(): return lax.ppermute(a, 'dp', [(i, i ^ bit) for i in range(count)])  60.4 us
    ppermute x42, waiting for transfers between devices, swap_dp(): return lax.ppermute(a, 'dp', [(i, i ^ bit) for i in range(count)])  57.7 us
    pallas_call x1, Pallas kernels, run_middle(): call(middle_kernel, count // tile, [rows(tile, width), rows(tile, width),...  38.6 us
    pallas_call x1, Pallas kernels, run_keys_back(): call(keys_back_kernel, count // tile, [rows(tile, wide), rows(tile, width...  15.8 us
    dot_general x5, matrix products, tn(): lax.dot_general(a, b, (((0,), (0,)), ((), ())), preferred_element_type=F32)  15.5 us
    pallas_call x1, Pallas kernels, run_attention_back(): call(attention_back_kernel, count // tile, [rows(tile, width), rows(tile,...  15.2 us
    pallas_call x1, Pallas kernels, run_queries_back(): call(queries_back_kernel, count // tile, [rows(tile, 2 * width), rows(til...  12.9 us
    pallas_call x1, Pallas kernels, run_keys(): call(keys_kernel, count // tile, [rows(tile, width), full(key_weight.shap...  12.4 us
  transfers between devices with their start and end apart: 48, of which 23 were waited for; matrix products, arithmetic and copies ran while one was open for 17% of the time, Pallas kernels for 16%

profile of v1, /device:TPU:0, one launch (start us, length us, event | category | flops | bytes accessed | tf_op | source)
XLA Modules:
  0.0 313.3 jit_solution(6356013971898077385)
XLA Ops:
  9.3 3.0 collective-permute-start.1
  15.7 2.4 constant_dynamic-slice_fusion.24
  21.5 2.0 collective-permute-start.6
  23.5 2.7 collective-permute-start.2
  29.2 4.9 %collective-permute-start.3 = (bf16[2,48,896]{2,1,0:T(8,128)(2,1)S(1)}, bf16[2,48,896]{2,1,0:T(8,128)(2,1)S(1)}, u32[]{:S(2)}, u32[]{:S(2)}) collective-permute-start(bf16[2,48,896]{2,1,0:T(8,128)(2,1)S(1)} %maximum_select_fusion.16), channel_id=1, source_target_pairs={{0,8},{2,10},{4,12},{6,14},{8,0},{10,2},{12,4},{14,6},{16,24},{18,... | collective-permute-start | bytes 516104 | tf_op jit(solution)/shard_map/ppermute | solution.py:65
  34.1 2.4 collective-permute-done.7
  39.3 6.3 %collective-permute-done.8 = bf16[2,2,48,768]{3,2,1,0:T(8,128)(2,1)S(1)} collective-permute-done((bf16[2,2,48,768]{3,2,1,0:T(8,128)(2,1)S(1)}, bf16[2,2,48,768]{3,2,1,0:T(8,128)(2,1)S(1)}, u32[]{:S(2)}, u32[]{:S(2)}) %collective-permute-start.8) | collective-permute-done | bytes 294944 | tf_op jit(solution)/shard_map/ppermute | solution.py:65
  50.1 12.4 %shard_map.263 = (bf16[1024,3072]{1,0:T(8,128)(2,1)}, bf16[1024,768]{1,0:T(8,128)(2,1)}, bf16[1024,768]{1,0:T(8,128)(2,1)}, bf16[784,256]{1,0:T(8,128)(2,1)}, bf16[5488,256]{1,0:T(8,128)(2,1)}) custom-call(s32[16]{0:T(128)} %pad_add_fusion.meta, bf16[1024,768]{1,0:T(8,128)(2,1)} %x.28, bf16[768,896]{1,0:T(8,128)(2,1)} %bitcast.142, ...), custom_call_target="tpu_custom_call" | custom-call | flops 10000000000 | bytes 20000000 | tf_op jit(solution)/shard_map/pallas_call | solution.py:766
  67.6 10.4 %collective-permute-done.11 = bf16[392,256]{1,0:T(8,128)(2,1)S(1)} collective-permute-done((bf16[392,256]{1,0:T(8,128)(2,1)S(1)}, bf16[392,256]{1,0:T(8,128)(2,1)S(1)}, u32[]{:S(2)}, u32[]{:S(2)}) %collective-permute-start.11) | collective-permute-done | bytes 200736 | tf_op jit(solution)/shard_map/ppermute | solution.py:65
  82.0 3.4 %collective-permute-done.17.down_here = bf16[768,768]{1,0:T(8,128)(2,1)} collective-permute-done((bf16[768,768]{1,0:T(8,128)(2,1)S(1)}, bf16[768,768]{1,0:T(8,128)(2,1)}, u32[]{:S(2)}, u32[]{:S(2)}) %collective-permute-start.17) | collective-permute-done | bytes 1179680 | tf_op jit(solution)/shard_map/ppermute | solution.py:69
  86.3 4.1 %collective-permute-start.13 = (bf16[392,256]{1,0:T(8,128)(2,1)S(1)}, bf16[392,256]{1,0:T(8,128)(2,1)S(1)}, u32[]{:S(2)}, u32[]{:S(2)}) collective-permute-start(bf16[392,256]{1,0:T(8,128)(2,1)S(1)} %add_convert_fusion.16), channel_id=1, source_target_pairs={{0,16},{2,18},{4,20},{6,22},{8,24},{10,26},{12,28},{14,30},{16,0},... | collective-permute-start | bytes 602120 | tf_op jit(solution)/shard_map/ppermute | solution.py:65
  90.4 8.7 %shard_map.264 = (bf16[1024,3072]{1,0:T(8,128)(2,1)}, bf16[1024,768]{1,0:T(8,128)(2,1)}, bf16[1024,384]{1,0:T(8,128)(2,1)}) custom-call(s32[16]{0:T(128)} %pad_add_fusion.meta, bf16[1024,768]{1,0:T(8,128)(2,1)} %x.28, bf16[768,1536]{1,0:T(8,128)(2,1)} %all-gather.2.cloned.1.call-done.weight.out_weight, f32[1,2304]{1,0:T(1,128)} %reshape.996.bias, ...), custom_call_target="tpu_custom_call" | custom-call | flops 6000000000 | bytes 20000000 | tf_op jit(solution)/shard_map/pallas_call | solution.py:796
  103.5 38.6 %shard_map.265 = (bf16[1024,768]{1,0:T(8,128)(2,1)}, f32[1024,768]{1,0:T(8,128)}, f32[1024,768]{1,0:T(8,128)}, f32[1024,128]{1,0:T(8,128)}, bf16[1024,768]{1,0:T...) custom-call(s32[16]{0:T(128)} %pad_add_fusion.meta, ...), custom_call_target="tpu_custom_call" | custom-call | flops 30000001024 | bytes 20000000 | tf_op jit(solution)/shard_map/pallas_call | solution.py:821
  142.1 15.2 %shard_map.266 = (f32[1024,768]{1,0:T(8,128)}, bf16[1024,768]{1,0:T(8,128)(2,1)}, bf16[1024,1536]{1,0:T(8,128)(2,1)}, bf16[1024,384]{1,0:T(8,128)(2,1)}, f32[24,...) custom-call(s32[16]{0:T(128)} %pad_add_fusion.meta, f32[1024,768]{1,0:T(8,128)} %get-tuple-element.110.hidden_grad, ...), custom_call_target="tpu_custom_call" | custom-call | flops 6000000000 | bytes 20000000 | tf_op jit(solution)/shard_map/pallas_call | solution.py:879
  158.8 2.9 convolution_convert_fusion.1
  163.4 5.1 %convolution_convert_fusion = bf16[768,1536]{1,0:T(8,128)(2,1)S(1)} fusion(bf16[1024,768]{1,0:T(8,128)(2,1)} %get-tuple-element.123, bf16[1024,1536]{1,0:T(8,128)(2,1)} %get-tuple-element.124), kind=kOutput, calls=%fused_computation.2 | convolution fusion | flops 2417098752 | bytes 7077888 | tf_op jit(solution)/shard_map/dot_general | solution.py:31
  171.8 3.3 %convolution_convert_fusion.4 = bf16[384,768]{1,0:T(8,128)(2,1)} fusion(bf16[1024,384]{1,0:T(8,128)(2,1)} %get-tuple-element.129, bf16[1024,768]{1,0:T(8,128)(2,1)} %get-tuple-element.130), kind=kOutput, calls=%fused_computation.20 | convolution fusion | flops 604274688 | bytes 2949120 | tf_op jit(solution)/shard_map/dot_general | solution.py:31
  179.2 15.6 %collective-permute-start.24 = (bf16[408,256]{1,0:T(8,128)(2,1)S(1)}, bf16[408,256]{1,0:T(8,128)(2,1)}, u32[]{:S(2)}, u32[]{:S(2)}) collective-permute-start(bf16[408,256]{1,0:T(8,128)(2,1)S(1)} %add_convert_fusion.14), channel_id=1, source_target_pairs={{0,16},{2,18},{4,20},{6,22},{8,24},{10,26},{12,28},{14,30},{16,0},... | collective-permute-start | bytes 626696 | tf_op jit(solution)/shard_map/ppermute | solution.py:65
  195.0 12.9 %shard_map.267 = (bf16[1024,768]{1,0:T(8,128)(2,1)}, f32[1024,768]{1,0:T(8,128)}, f32[8,768]{1,0:T(8,128)}) custom-call(s32[16]{0:T(128)} %pad_add_fusion.meta, bf16[1024,1536]{1,0:T(8,128)(2,1)} %get-tuple-element.133.mixed, bf16[1024,3072]{1,0:T(8,128)(2,1)} %get-tuple-element.97.phi, bf16[1024,768]{1,0:T(8,128)(2,1)} %get-tuple-element.134.scaled, ...), custom_call_target="tpu_custom_call" | custom-call | flops 8000000000 | bytes 20000000 | tf_op jit(solution)/shard_map/pallas_call | solution.py:911
  224.8 2.0 collective-permute-done.30
  227.8 4.6 %collective-permute-start.33 = (bf16[96,1536]{1,0:T(8,128)(2,1)S(1)}, bf16[96,1536]{1,0:T(8,128)(2,1)S(1)}, u32[]{:S(2)}, u32[]{:S(2)}) collective-permute-start(bf16[96,1536]{1,0:T(8,128)(2,1)S(1)} %add_convert_fusion.10), channel_id=1, source_target_pairs={{0,16},{2,18},{4,20},{6,22},{8,24},{10,26},{12,28},{14,30},{16,0},... | collective-permute-start | bytes 884744 | tf_op jit(solution)/shard_map/ppermute | solution.py:65
  232.6 15.8 %shard_map.268 = (bf16[1024,1536]{1,0:T(8,128)(2,1)}, bf16[1024,768]{1,0:T(8,128)(2,1)}, f32[8,1536]{1,0:T(8,128)}) custom-call(s32[16]{0:T(128)} %pad_add_fusion.meta, bf16[1024,3072]{1,0:T(8,128)(2,1)} %get-tuple-element.107.phi, bf16[1024,768]{1,0:T(8,128)(2,1)} %get-tuple-element.108.values, bf16[1024,768]{1,0:T(8,128)(2,1)} %get-tuple-element.109.scaled, ...), custom_call_target="tpu_custom_call" | custom-call | flops 12000000000 | bytes 20000000 | tf_op jit(solution)/shard_map/pallas_call | solution.py:937
  250.3 1.9 collective-permute-start.37
  252.5 3.3 %convolution_convert_fusion.2 = bf16[384,1536]{1,0:T(8,128)(2,1)S(1)} fusion(bf16[1024,384]{1,0:T(8,128)(2,1)S(1)} %copy-done.6, bf16[1024,1536]{1,0:T(8,128)(2,1)} %get-tuple-element.155), kind=kOutput, calls=%fused_computation.8 | convolution fusion | flops 1208549376 | bytes 5111808 | tf_op jit(solution)/shard_map/dot_general | solution.py:31
  257.0 7.8 %collective-permute-done.32 = bf16[96,1536]{1,0:T(8,128)(2,1)S(1)} collective-permute-done((bf16[96,1536]{1,0:T(8,128)(2,1)S(1)}, bf16[96,1536]{1,0:T(8,128)(2,1)S(1)}, u32[]{:S(2)}, u32[]{:S(2)}) %collective-permute-start.32) | collective-permute-done | bytes 294944 | tf_op jit(solution)/shard_map/ppermute | solution.py:65
  271.7 5.0 %collective-permute-done.42 = bf16[96,1664]{1,0:T(8,128)(2,1)S(1)} collective-permute-done((bf16[96,1664]{1,0:T(8,128)(2,1)S(1)}, bf16[96,1664]{1,0:T(8,128)(2,1)S(1)}, u32[]{:S(2)}, u32[]{:S(2)}) %collective-permute-start.42) | collective-permute-done | bytes 319520 | tf_op jit(solution)/shard_map/ppermute | solution.py:65
  278.0 8.4 %collective-permute-done.41 = bf16[384,768]{1,0:T(8,128)(2,1)S(1)} collective-permute-done((bf16[384,768]{1,0:T(8,128)(2,1)S(1)}, bf16[384,768]{1,0:T(8,128)(2,1)S(1)}, u32[]{:S(2)}, u32[]{:S(2)}) %collective-permute-start.41) | collective-permute-done | bytes 589856 | tf_op jit(solution)/shard_map/ppermute | solution.py:65
  287.9 4.1 %collective-permute-start.44 = (bf16[24,1664]{1,0:T(8,128)(2,1)S(1)}, bf16[24,1664]{1,0:T(8,128)(2,1)S(1)}, u32[]{:S(2)}, u32[]{:S(2)}) collective-permute-start(bf16[24,1664]{1,0:T(8,128)(2,1)S(1)} %constant_dynamic-slice_fusion.1), channel_id=1, source_target_pairs={{0,16},{2,18},{4,20},{6,22},{8,24},{10,26},{12,28},{14,30},{16,0},... | collective-permute-start | bytes 239624 | tf_op jit(solution)/shard_map/ppermute | solution.py:65
  292.6 3.8 %collective-permute-done.44 = bf16[24,1664]{1,0:T(8,128)(2,1)S(1)} collective-permute-done((bf16[24,1664]{1,0:T(8,128)(2,1)S(1)}, bf16[24,1664]{1,0:T(8,128)(2,1)S(1)}, u32[]{:S(2)}, u32[]{:S(2)}) %collective-permute-start.44) | collective-permute-done | bytes 79904 | tf_op jit(solution)/shard_map/ppermute | solution.py:65
  297.8 2.0 maximum_select_fusion.1
  299.8 3.0 bitcast_convert_fusion
  303.2 2.7 bitcast_convert_fusion.1
  (242 shorter events, 77.1 us)
Async XLA Ops:
  7.2 83.2 %all-gather.2.cloned.1.call-start = ((), (), s32[]{:S(2)}) async-start(), calls=%async_computation | async-start | bytes 2433024 | tf_op jit(solution)/shard_map/all_gather | solution.py:1007
  9.3 12.1 %collective-permute-start.1 = (bf16[24,128]{1,0:T(8,128)(2,1)S(1)}, bf16[24,128]{1,0:T(8,128)(2,1)S(1)}, u32[]{:S(2)}, u32[]{:S(2)}) collective-permute-start(bf16[24,128]{1,0:T(8,128)(2,1)S(1)} %get-tuple-element.221), channel_id=1, source_target_pairs={{0,1},{1,0},{2,3},{3,2},{4,5},{5,4},{6,7},{7,6},{8,9},{9,8},{10,11... | collective-permute-start | bytes 18440 | tf_op jit(solution)/shard_map/ppermute | solution.py:69
  12.3 9.1 %collective-permute-start = (bf16[24,2304]{1,0:T(8,128)(2,1)}, bf16[24,2304]{1,0:T(8,128)(2,1)S(1)}, u32[]{:S(2)}, u32[]{:S(2)}) collective-permute-start(bf16[24,2304]{1,0:T(8,128)(2,1)} %param.19), channel_id=1, source_target_pairs={{0,1},{1,0},{2,3},{3,2},{4,5},{5,4},{6,7},{7,6},{8,9},{9,8},{10,11... | collective-permute-start | bytes 331784 | tf_op jit(solution)/shard_map/ppermute | solution.py:69
  26.2 36.3 %collective-permute-start.15 = (bf16[384,1536]{1,0:T(8,128)(2,1)}, bf16[384,1536]{1,0:T(8,128)(2,1)}, u32[]{:S(2)}, u32[]{:S(2)}) collective-permute-start(bf16[384,1536]{1,0:T(8,128)(2,1)} %constant_dynamic-slice_fusion.24), channel_id=1, source_target_pairs={{0,1},{1,0},{2,3},{3,2},{4,5},{5,4},{6,7},{7,6},{8,9},{9,8},{10,11... | collective-permute-start | bytes 3538952 | tf_op jit(solution)/shard_map/ppermute | solution.py:69
  27.8 57.6 %collective-permute-start.17 = (bf16[768,768]{1,0:T(8,128)(2,1)S(1)}, bf16[768,768]{1,0:T(8,128)(2,1)}, u32[]{:S(2)}, u32[]{:S(2)}) collective-permute-start(bf16[768,768]{1,0:T(8,128)(2,1)S(1)} %constant_dynamic-slice_fusion.23), channel_id=1, source_target_pairs={{0,1},{1,0},{2,3},{3,2},{4,5},{5,4},{6,7},{7,6},{8,9},{9,8},{10,11... | collective-permute-start | bytes 3538952 | tf_op jit(solution)/shard_map/ppermute | solution.py:69
  28.3 8.2 %collective-permute-start.7 = (bf16[2,48,768]{2,1,0:T(8,128)(2,1)S(1)}, bf16[2,48,768]{2,1,0:T(8,128)(2,1)S(1)}, u32[]{:S(2)}, u32[]{:S(2)}) collective-permute-start(bf16[2,48,768]{2,1,0:T(8,128)(2,1)S(1)} %maximum_select_fusion.18), channel_id=1, source_target_pairs={{0,16},{2,18},{4,20},{6,22},{8,24},{10,26},{12,28},{14,30},{16,0},... | collective-permute-start | bytes 442376 | tf_op jit(solution)/shard_map/ppermute | solution.py:65
  29.2 9.8 %collective-permute-start.3 = (bf16[2,48,896]{2,1,0:T(8,128)(2,1)S(1)}, bf16[2,48,896]{2,1,0:T(8,128)(2,1)S(1)}, u32[]{:S(2)}, u32[]{:S(2)}) collective-permute-start(bf16[2,48,896]{2,1,0:T(8,128)(2,1)S(1)} %maximum_select_fusion.16), channel_id=1, source_target_pairs={{0,8},{2,10},{4,12},{6,14},{8,0},{10,2},{12,4},{14,6},{16,24},{18,... | collective-permute-start | bytes 516104 | tf_op jit(solution)/shard_map/ppermute | solution.py:65
  36.6 9.0 %collective-permute-start.8 = (bf16[2,2,48,768]{3,2,1,0:T(8,128)(2,1)S(1)}, bf16[2,2,48,768]{3,2,1,0:T(8,128)(2,1)S(1)}, u32[]{:S(2)}, u32[]{:S(2)}) collective-permute-start(bf16[2,2,48,768]{3,2,1,0:T(8,128)(2,1)S(1)} %maximum_select_fusion.14), channel_id=1, source_target_pairs={{0,8},{2,10},{4,12},{6,14},{8,0},{10,2},{12,4},{14,6},{16,24},{18,... | collective-permute-start | bytes 884744 | tf_op jit(solution)/shard_map/ppermute | solution.py:65
  62.5 22.9 %collective-permute-start.16 = (bf16[384,1536]{1,0:T(8,128)(2,1)}, bf16[384,1536]{1,0:T(8,128)(2,1)}, u32[]{:S(2)}, u32[]{:S(2)}) collective-permute-start(bf16[384,1536]{1,0:T(8,128)(2,1)} %collective-permute-done.15.up_here), channel_id=1, source_target_pairs={{0,2},{2,0},{4,6},{6,4},{8,10},{10,8},{12,14},{14,12},{16,18},{18,... | collective-permute-start | bytes 3538952 | tf_op jit(solution)/shard_map/ppermute | solution.py:65
  66.7 11.3 %collective-permute-start.11 = (bf16[392,256]{1,0:T(8,128)(2,1)S(1)}, bf16[392,256]{1,0:T(8,128)(2,1)S(1)}, u32[]{:S(2)}, u32[]{:S(2)}) collective-permute-start(bf16[392,256]{1,0:T(8,128)(2,1)S(1)} %fusion.10), channel_id=1, source_target_pairs={{0,4},{2,6},{4,0},{6,2},{8,12},{10,14},{12,8},{14,10},{16,20},{18,... | collective-permute-start | bytes 602120 | tf_op jit(solution)/shard_map/ppermute | solution.py:65
  80.5 20.5 %collective-permute-start.19 = (bf16[1,1536]{1,0:T(2,128)(2,1)S(1)}, bf16[1,1536]{1,0:T(2,128)(2,1)S(1)}, u32[]{:S(2)}, u32[]{:S(2)}) collective-permute-start(bf16[1,1536]{1,0:T(2,128)(2,1)S(1)} %broadcast_in_dim.5), channel_id=1, source_target_pairs={{0,1},{1,0},{2,3},{3,2},{4,5},{5,4},{6,7},{7,6},{8,9},{9,8},{10,11... | collective-permute-start | bytes 9224 | tf_op jit(solution)/shard_map/ppermute | solution.py:69
  85.4 17.1 %collective-permute-start.18 = (bf16[768,768]{1,0:T(8,128)(2,1)}, bf16[768,768]{1,0:T(8,128)(2,1)S(1)}, u32[]{:S(2)}, u32[]{:S(2)}) collective-permute-start(bf16[768,768]{1,0:T(8,128)(2,1)} %collective-permute-done.17.down_here), channel_id=1, source_target_pairs={{0,2},{2,0},{4,6},{6,4},{8,10},{10,8},{12,14},{14,12},{16,18},{18,... | collective-permute-start | bytes 3538952 | tf_op jit(solution)/shard_map/ppermute | solution.py:65
  86.3 13.4 %collective-permute-start.13 = (bf16[392,256]{1,0:T(8,128)(2,1)S(1)}, bf16[392,256]{1,0:T(8,128)(2,1)S(1)}, u32[]{:S(2)}, u32[]{:S(2)}) collective-permute-start(bf16[392,256]{1,0:T(8,128)(2,1)S(1)} %add_convert_fusion.16), channel_id=1, source_target_pairs={{0,16},{2,18},{4,20},{6,22},{8,24},{10,26},{12,28},{14,30},{16,0},... | collective-permute-start | bytes 602120 | tf_op jit(solution)/shard_map/ppermute | solution.py:65
  176.0 35.3 %collective-permute-start.27 = (bf16[384,768]{1,0:T(8,128)(2,1)}, bf16[384,768]{1,0:T(8,128)(2,1)}, u32[]{:S(2)}, u32[]{:S(2)}) collective-permute-start(bf16[384,768]{1,0:T(8,128)(2,1)} %constant_dynamic-slice_fusion.18), channel_id=1, source_target_pairs={{0,4},{2,6},{4,0},{6,2},{8,12},{10,14},{12,8},{14,10},{16,20},{18,... | collective-permute-start | bytes 1769480 | tf_op jit(solution)/shard_map/ppermute | solution.py:65
  179.2 29.4 %collective-permute-start.24 = (bf16[408,256]{1,0:T(8,128)(2,1)S(1)}, bf16[408,256]{1,0:T(8,128)(2,1)}, u32[]{:S(2)}, u32[]{:S(2)}) collective-permute-start(bf16[408,256]{1,0:T(8,128)(2,1)S(1)} %add_convert_fusion.14), channel_id=1, source_target_pairs={{0,16},{2,18},{4,20},{6,22},{8,24},{10,26},{12,28},{14,30},{16,0},... | collective-permute-start | bytes 626696 | tf_op jit(solution)/shard_map/ppermute | solution.py:65
  194.9 19.0 %collective-permute-start.26 = (bf16[192,1536]{1,0:T(8,128)(2,1)S(1)}, bf16[192,1536]{1,0:T(8,128)(2,1)S(1)}, u32[]{:S(2)}, u32[]{:S(2)}) collective-permute-start(bf16[192,1536]{1,0:T(8,128)(2,1)S(1)} %get-tuple-element.180), channel_id=1, source_target_pairs={{0,8},{2,10},{4,12},{6,14},{8,0},{10,2},{12,4},{14,6},{16,24},{18,... | collective-permute-start | bytes 1769480 | tf_op jit(solution)/shard_map/ppermute | solution.py:65
  216.2 16.2 %collective-permute-start.29 = (bf16[192,1536]{1,0:T(8,128)(2,1)S(1)}, bf16[192,1536]{1,0:T(8,128)(2,1)S(1)}, u32[]{:S(2)}, u32[]{:S(2)}) collective-permute-start(bf16[192,1536]{1,0:T(8,128)(2,1)S(1)} %get-tuple-element.178), channel_id=1, source_target_pairs={{0,2},{2,0},{4,6},{6,4},{8,10},{10,8},{12,14},{14,12},{16,18},{18,... | collective-permute-start | bytes 1769480 | tf_op jit(solution)/shard_map/ppermute | solution.py:65
  217.5 9.3 %collective-permute-start.30 = (bf16[96,1536]{1,0:T(8,128)(2,1)}, bf16[96,1536]{1,0:T(8,128)(2,1)}, u32[]{:S(2)}, u32[]{:S(2)}) collective-permute-start(bf16[96,1536]{1,0:T(8,128)(2,1)} %constant_dynamic-slice_fusion.15), channel_id=1, source_target_pairs={{0,4},{2,6},{4,0},{6,2},{8,12},{10,14},{12,8},{14,10},{16,20},{18,... | collective-permute-start | bytes 884744 | tf_op jit(solution)/shard_map/ppermute | solution.py:65
  220.2 28.2 %collective-permute-start.34 = (bf16[192,768]{1,0:T(8,128)(2,1)S(1)}, bf16[192,768]{1,0:T(8,128)(2,1)}, u32[]{:S(2)}, u32[]{:S(2)}) collective-permute-start(bf16[192,768]{1,0:T(8,128)(2,1)S(1)} %add_convert_fusion.11), channel_id=1, source_target_pairs={{0,16},{2,18},{4,20},{6,22},{8,24},{10,26},{12,28},{14,30},{16,0},... | collective-permute-start | bytes 884744 | tf_op jit(solution)/shard_map/ppermute | solution.py:65
  227.8 21.9 %collective-permute-start.33 = (bf16[96,1536]{1,0:T(8,128)(2,1)S(1)}, bf16[96,1536]{1,0:T(8,128)(2,1)S(1)}, u32[]{:S(2)}, u32[]{:S(2)}) collective-permute-start(bf16[96,1536]{1,0:T(8,128)(2,1)S(1)} %add_convert_fusion.10), channel_id=1, source_target_pairs={{0,16},{2,18},{4,20},{6,22},{8,24},{10,26},{12,28},{14,30},{16,0},... | collective-permute-start | bytes 884744 | tf_op jit(solution)/shard_map/ppermute | solution.py:65
  249.7 18.6 %collective-permute-start.36 = (bf16[96,1536]{1,0:T(8,128)(2,1)S(1)}, bf16[96,1536]{1,0:T(8,128)(2,1)S(1)}, u32[]{:S(2)}, u32[]{:S(2)}) collective-permute-start(bf16[96,1536]{1,0:T(8,128)(2,1)S(1)} %add_convert_fusion.8), channel_id=1, source_target_pairs={{0,4},{2,6},{4,0},{6,2},{8,12},{10,14},{12,8},{14,10},{16,20},{18,... | collective-permute-start | bytes 884744 | tf_op jit(solution)/shard_map/ppermute | solution.py:65
  250.3 17.1 %collective-permute-start.37 = (bf16[192,768]{1,0:T(8,128)(2,1)S(1)}, bf16[192,768]{1,0:T(8,128)(2,1)S(1)}, u32[]{:S(2)}, u32[]{:S(2)}) collective-permute-start(bf16[192,768]{1,0:T(8,128)(2,1)S(1)} %add_convert_fusion.9), channel_id=1, source_target_pairs={{0,8},{2,10},{4,12},{6,14},{8,0},{10,2},{12,4},{14,6},{16,24},{18,... | collective-permute-start | bytes 884744 | tf_op jit(solution)/shard_map/ppermute | solution.py:65
  255.8 9.0 %collective-permute-start.32 = (bf16[96,1536]{1,0:T(8,128)(2,1)S(1)}, bf16[96,1536]{1,0:T(8,128)(2,1)S(1)}, u32[]{:S(2)}, u32[]{:S(2)}) collective-permute-start(bf16[96,1536]{1,0:T(8,128)(2,1)S(1)} %get-tuple-element.186), channel_id=1, source_target_pairs={{0,4},{2,6},{4,0},{6,2},{8,12},{10,14},{12,8},{14,10},{16,20},{18,... | collective-permute-start | bytes 884744 | tf_op jit(solution)/shard_map/ppermute | solution.py:65
  256.9 8.9 %collective-permute-start.38 = (bf16[192,1664]{1,0:T(8,128)(2,1)S(1)}, bf16[192,1664]{1,0:T(8,128)(2,1)S(1)}, u32[]{:S(2)}, u32[]{:S(2)}) collective-permute-start(bf16[192,1664]{1,0:T(8,128)(2,1)S(1)} %get-tuple-element.177), channel_id=1, source_target_pairs={{0,2},{2,0},{4,6},{6,4},{8,10},{10,8},{12,14},{14,12},{16,18},{18,... | collective-permute-start | bytes 1916936 | tf_op jit(solution)/shard_map/ppermute | solution.py:65
  266.1 10.5 %collective-permute-start.42 = (bf16[96,1664]{1,0:T(8,128)(2,1)S(1)}, bf16[96,1664]{1,0:T(8,128)(2,1)S(1)}, u32[]{:S(2)}, u32[]{:S(2)}) collective-permute-start(bf16[96,1664]{1,0:T(8,128)(2,1)S(1)} %get-tuple-element.185), channel_id=1, source_target_pairs={{0,4},{2,6},{4,0},{6,2},{8,12},{10,14},{12,8},{14,10},{16,20},{18,... | collective-permute-start | bytes 958472 | tf_op jit(solution)/shard_map/ppermute | solution.py:65
  267.5 19.0 %collective-permute-start.41 = (bf16[384,768]{1,0:T(8,128)(2,1)S(1)}, bf16[384,768]{1,0:T(8,128)(2,1)S(1)}, u32[]{:S(2)}, u32[]{:S(2)}) collective-permute-start(bf16[384,768]{1,0:T(8,128)(2,1)S(1)} %bitcast.139), channel_id=1, source_target_pairs={{0,4},{2,6},{4,0},{6,2},{8,12},{10,14},{12,8},{14,10},{16,20},{18,... | collective-permute-start | bytes 1769480 | tf_op jit(solution)/shard_map/ppermute | solution.py:65
  268.5 18.3 %collective-permute-start.40 = (bf16[192,1536]{1,0:T(8,128)(2,1)S(1)}, bf16[192,1536]{1,0:T(8,128)(2,1)S(1)}, u32[]{:S(2)}, u32[]{:S(2)}) collective-permute-start(bf16[192,1536]{1,0:T(8,128)(2,1)S(1)} %bitcast.137), channel_id=1, source_target_pairs={{0,8},{2,10},{4,12},{6,14},{8,0},{10,2},{12,4},{14,6},{16,24},{18,... | collective-permute-start | bytes 1769480 | tf_op jit(solution)/shard_map/ppermute | solution.py:65
  271.6 20.3 %collective-permute-start.39 = (bf16[24,1536]{1,0:T(8,128)(2,1)S(1)}, bf16[24,1536]{1,0:T(8,128)(2,1)S(1)}, u32[]{:S(2)}, u32[]{:S(2)}) collective-permute-start(bf16[24,1536]{1,0:T(8,128)(2,1)S(1)} %constant_dynamic-slice_fusion.6), channel_id=1, source_target_pairs={{0,16},{2,18},{4,20},{6,22},{8,24},{10,26},{12,28},{14,30},{16,0},... | collective-permute-start | bytes 221192 | tf_op jit(solution)/shard_map/ppermute | solution.py:65
  276.8 11.0 %collective-permute-start.43 = (bf16[48,1664]{1,0:T(8,128)(2,1)S(1)}, bf16[48,1664]{1,0:T(8,128)(2,1)S(1)}, u32[]{:S(2)}, u32[]{:S(2)}) collective-permute-start(bf16[48,1664]{1,0:T(8,128)(2,1)S(1)} %get-tuple-element.197), channel_id=1, source_target_pairs={{0,8},{2,10},{4,12},{6,14},{8,0},{10,2},{12,4},{14,6},{16,24},{18,... | collective-permute-start | bytes 479240 | tf_op jit(solution)/shard_map/ppermute | solution.py:65
  286.7 16.2 %collective-permute-start.46 = (bf16[768,768]{1,0:T(8,128)(2,1)S(1)}, bf16[768,768]{1,0:T(8,128)(2,1)S(1)}, u32[]{:S(2)}, u32[]{:S(2)}) collective-permute-start(bf16[768,768]{1,0:T(8,128)(2,1)S(1)} %bitcast.132), channel_id=1, source_target_pairs={{0,2},{2,0},{4,6},{6,4},{8,10},{10,8},{12,14},{14,12},{16,18},{18,... | collective-permute-start | bytes 3538952 | tf_op jit(solution)/shard_map/ppermute | solution.py:65
  286.9 10.9 %collective-permute-start.45 = (bf16[384,1536]{1,0:T(8,128)(2,1)S(1)}, bf16[384,1536]{1,0:T(8,128)(2,1)}, u32[]{:S(2)}, u32[]{:S(2)}) collective-permute-start(bf16[384,1536]{1,0:T(8,128)(2,1)S(1)} %bitcast.134), channel_id=1, source_target_pairs={{0,2},{2,0},{4,6},{6,4},{8,10},{10,8},{12,14},{14,12},{16,18},{18,... | collective-permute-start | bytes 3538952 | tf_op jit(solution)/shard_map/ppermute | solution.py:65
  287.9 8.6 %collective-permute-start.44 = (bf16[24,1664]{1,0:T(8,128)(2,1)S(1)}, bf16[24,1664]{1,0:T(8,128)(2,1)S(1)}, u32[]{:S(2)}, u32[]{:S(2)}) collective-permute-start(bf16[24,1664]{1,0:T(8,128)(2,1)S(1)} %constant_dynamic-slice_fusion.1), channel_id=1, source_target_pairs={{0,16},{2,18},{4,20},{6,22},{8,24},{10,26},{12,28},{14,30},{16,0},... | collective-permute-start | bytes 239624 | tf_op jit(solution)/shard_map/ppermute | solution.py:65
  (33 other events, 219.8 us)
Sparse Core Ops, SparseCore 0:
  26.3 60.4 all-gather.1
